TPU v7x, 256 devices: a whole 4x4x8 slice. The times are simulated.
256 devices in a mesh: view: 32 (over x, z), head: 8 (over y, core).
Axes of the slice: x: 4, y: 4, z: 8, core: 2. Of those that a mesh axis runs over, the one named last changes fastest.
Arguments:
- features: bfloat16 [65536, 1024], P(('view', 'head')), may hold values from -6 to 6
- attend_weight: bfloat16 [2, 3, 1024, 1024], P(None, None, 'view', 'head'), may hold values from -0.1875 to 0.1875
- output_weight: bfloat16 [2, 1024, 1024], P(None, 'view'), may hold values from -0.1875 to 0.1875
- fast_init: bfloat16 [2, 16, 3, 64, 512], P(None, 'head', None, None, 'view'), may hold values from -0.75 to 0.75
- update_mask: int32 [32, 2048], P('view'), may hold values 0 or 1
Outputs:
- refined: bfloat16 [65536, 1024], P(('view', 'head'))
All inputs are finite; a program needn't handle non-finite values. No bound on the sum of `update_mask` on one device may be relied on, other than what follows from the above.
Results may differ from a plain program's by a relative error of at most 0.035.
Values may be sent and summed in bfloat16 or wider, within the bound.
A program may use at most 64 MiB of HBM per device.

v0:
```python
import jax
import jax.numpy as jnp
from jax import lax
from jax.sharding import PartitionSpec as P

BLOCKS = 2
NS_STEPS = 5


newton_coeffs = (3.4445, -4.775, 2.0315)
learn_rate = 1.0
score_scale = 0.25


def normalize(values, epsilon):
    return values * lax.rsqrt(jnp.mean(values * values, axis=-1, keepdims=True) + epsilon)


def newton_step(current, gram_matrix):
    squared = jnp.einsum(
        "...de,...ef->...df", gram_matrix, gram_matrix, precision=lax.Precision.HIGHEST
    )
    polynomial = newton_coeffs[1] * gram_matrix + newton_coeffs[2] * squared
    return newton_coeffs[0] * current + jnp.einsum(
        "...de,...ef->...df", polynomial, current, precision=lax.Precision.HIGHEST
    )


def self_gram(current):
    return jnp.einsum("...df,...ef->...de", current, current, precision=lax.Precision.HIGHEST)


def fast_gradient(keys, values, mask, weights):
    first = jnp.einsum("thd,hdf->thf", keys, weights[:, 0], preferred_element_type=jnp.float32)
    third = jnp.einsum("thd,hdf->thf", keys, weights[:, 1], preferred_element_type=jnp.float32)
    sigma = jax.nn.sigmoid(first)
    hidden = (first * sigma * third).astype(jnp.bfloat16)
    target = (-(mask[:, None, None].astype(jnp.float32) * values.astype(jnp.float32))).astype(
        jnp.bfloat16
    )
    back = jnp.einsum("thd,hdf->thf", target, weights[:, 2], preferred_element_type=jnp.float32)
    d_third = (back * first * sigma).astype(jnp.bfloat16)
    d_first = (back * third * sigma * (1.0 + first * (1.0 - sigma))).astype(jnp.bfloat16)
    grad_first = jnp.einsum("thd,thf->hdf", keys, d_first, preferred_element_type=jnp.float32)
    grad_third = jnp.einsum("thd,thf->hdf", keys, d_third, preferred_element_type=jnp.float32)
    grad_last = jnp.einsum("thd,thf->hdf", target, hidden, preferred_element_type=jnp.float32)
    return jnp.stack([grad_first, grad_third, grad_last], axis=1)


def fast_apply(queries, weights):
    first = jnp.einsum("thd,hdf->thf", queries, weights[:, 0], preferred_element_type=jnp.float32)
    third = jnp.einsum("thd,hdf->thf", queries, weights[:, 1], preferred_element_type=jnp.float32)
    hidden = (first * jax.nn.sigmoid(first) * third).astype(jnp.bfloat16)
    output = jnp.einsum("thf,hdf->thd", hidden, weights[:, 2], preferred_element_type=jnp.float32)
    return normalize(output, 1e-05)


def shards(features, attend_weight, output_weight, fast_init, update_mask):
    stream = features
    view_dev, view_len = update_mask.shape
    heads_here = fast_init.shape[1]
    head_dim = fast_init.shape[3]
    rows_all = view_dev * view_len
    block = min(512, view_len)
    count = rows_all // block
    mask_blocks = update_mask.reshape(count, block)
    for layer in range(BLOCKS):
        normed = normalize(stream.astype(jnp.float32), 1e-05).astype(jnp.bfloat16)
        columns = lax.all_gather(attend_weight[layer], "head", axis=2, tiled=True)
        packed = jnp.einsum(
            "td,jdc->tjc",
            normed,
            lax.all_gather(columns, "view", axis=1, tiled=True),
            preferred_element_type=jnp.float32,
        ).astype(jnp.bfloat16)
        packed = lax.all_to_all(packed, "head", split_axis=2, concat_axis=0, tiled=True)
        packed = packed.reshape(rows_all, 3, heads_here, head_dim)
        queries = normalize(packed[:, 0].astype(jnp.float32), 1e-05).astype(jnp.bfloat16)
        keys = normalize(packed[:, 1].astype(jnp.float32), 1e-05).astype(jnp.bfloat16)
        values = packed[:, 2]
        key_views = keys.reshape(view_dev, view_len, heads_here, head_dim)
        value_views = values.reshape(view_dev, view_len, heads_here, head_dim)
        query_blocks = jnp.moveaxis(
            queries.reshape(view_dev, view_len // block, block, heads_here, head_dim), 1, 0
        )

        def attend_block(query_block):
            scores = (
                jnp.einsum(
                    "vqhd,vkhd->vhqk", query_block, key_views, preferred_element_type=jnp.float32
                )
                * score_scale
            )
            expo = jnp.exp(scores)
            probs = (expo / jnp.sum(expo, axis=-1, keepdims=True)).astype(jnp.bfloat16)
            return jnp.einsum(
                "vhqk,vkhd->vqhd", probs, value_views, preferred_element_type=jnp.float32
            )

        attended = jnp.moveaxis(lax.map(attend_block, query_blocks), 0, 1).reshape(
            rows_all, heads_here, head_dim
        )
        local_fast = fast_init[layer]
        full_fast = lax.all_gather(local_fast, "view", axis=3, tiled=True)

        def accumulate(total, inputs):
            return (total + fast_gradient(inputs[0], inputs[1], inputs[2], full_fast), None)

        key_blocks = keys.reshape(count, block, heads_here, head_dim)
        value_blocks = values.reshape(count, block, heads_here, head_dim)
        gradients, _ = lax.scan(
            accumulate,
            jnp.zeros(full_fast.shape, jnp.float32),
            (key_blocks, value_blocks, mask_blocks),
        )
        summed = lax.psum(gradients.astype(jnp.bfloat16), "view").astype(jnp.float32)
        squares = jnp.sum(summed * summed, axis=(2, 3), keepdims=True)
        current = summed * lax.rsqrt(squares + 1e-06)
        for _ in range(NS_STEPS):
            current = newton_step(current, self_gram(current))
        updated = (full_fast.astype(jnp.float32) - learn_rate * current).astype(jnp.bfloat16)

        def apply_block(query_block):
            return fast_apply(query_block, updated)

        applied = lax.map(apply_block, queries.reshape(count, block, heads_here, head_dim)).reshape(
            rows_all, heads_here, head_dim
        )
        mixed = (attended + applied).astype(jnp.bfloat16).reshape(rows_all, heads_here * head_dim)
        regrouped = lax.all_to_all(mixed, "head", split_axis=0, concat_axis=1, tiled=True)
        projected = jnp.dot(
            regrouped,
            lax.all_gather(output_weight[layer], "view", axis=0, tiled=True),
            preferred_element_type=jnp.float32,
        )
        stream = (stream.astype(jnp.float32) + projected).astype(jnp.bfloat16)
    return stream


def solution(mesh):
    return jax.shard_map(
        shards,
        mesh=mesh,
        in_specs=(
            P(("view", "head"), None),
            P(None, None, "view", "head"),
            P(None, "view", None),
            P(None, "head", None, None, "view"),
            P("view", None),
        ),
        out_specs=P(("view", "head"), None),
        check_vma=False,
    )
```

profile of v0, /device:TPU:1, one launch (start us, length us, event | category | flops | bytes accessed | tf_op | source)
XLA Modules:
  0.0 899.8 jit_solution(528718162271528605)
XLA Ops:
  7.3 15.3 %all-gather = bf16[1,3,32,1024]{3,2,1,0:T(8,128)(2,1)} all-gather(bf16[1,3,32,128]{3,2,1,0:T(8,128)(2,1)S(1)} %get-tuple-element.359), channel_id=2, replica_groups=mesh['view'=32,'head'=8] {'head'}, dimensions={3}, use_global_device_ids=true | all-gather | bytes 221184 | tf_op jit(solution)/shard_map/all_gather | solution.py:69
  23.8 88.0 %all-gather.13.cloned.1.call-done = bf16[1,3,1024,1024]{3,2,1,0:T(8,128)(2,1)} async-done(((bf16[1,3,32,1024]{3,2,1,0:T(8,128)(2,1)}), bf16[1,3,1024,1024]{3,2,1,0:T(8,128)(2,1)}) %all-gather.13.cloned.1.call-update) | async-done | bytes 6291472 | tf_op jit(solution)/shard_map/all_gather | solution.py:73
  125.4 39.0 %all-gather.2 = bf16[1,2,3,64,512]{3,1,2,0,4:T(2,128)(2,1)S(1)} all-gather(bf16[1,2,3,64,16]{3,1,2,0,4:T(2,128)(2,1)S(1)} %copy.86), channel_id=4, replica_groups=mesh['view'=32,'head'=8] {'view'}, dimensions={4}, use_global_device_ids=true | all-gather | bytes 405504 | tf_op jit(solution)/shard_map/all_gather | solution.py:104
  184.0 47.7 %while.66 = (s32[]{:T(128)}, f32[2,3,64,512]{3,2,0,1:T(8,128)S(1)}, bf16[4,512,2,64]{1,3,2,0:T(8,128)(2,1)}, s32[4,512]{1,0:T(4,128)}, bf16[4,512,2,64]{1,3,2,0:...) while((s32[]{:T(128)}, f32[2,3,64,512]{3,2,0,1:T(8,128)S(1)}, ...), condition=%wide.region_7.8_spmd.clone, body=%wide.region_6.7_spmd.clone.sunk | while | flops 415498752 | bytes 25308256 | solution.py:111
  234.3 23.1 %all-gather.4 = bf16[1,3,32,1024]{3,2,1,0:T(8,128)(2,1)} all-gather(bf16[1,3,32,128]{3,2,1,0:T(8,128)(2,1)S(1)} %get-tuple-element.360), channel_id=6, replica_groups=mesh['view'=32,'head'=8] {'head'}, dimensions={3}, use_global_device_ids=true | all-gather | bytes 221184 | tf_op jit(solution)/shard_map/all_gather | solution.py:69
  262.5 28.7 %while.62 = (s32[]{:T(128)}, f32[4,1,512,2,64]{2,0,4,3,1:T(4,128)S(1)}, bf16[4,1,512,2,64]{2,4,3,1,0:T(8,128)(2,1)}, bf16[1,2048,2,64]{1,3,2,0:T(8,128)(2,1)S(1)...) while((s32[]{:T(128)}, f32[4,1,512,2,64]{2,0,4,3,1:T(4,128)S(1)}, ...), condition=%wide.region_5.6_spmd, body=%wide.region_3.5_spmd.sunk | while | flops 547355648 | bytes 21373548 | solution.py:100
  295.8 84.2 %all-reduce.3.cloned.1.call-done = bf16[2,3,64,512]{3,2,1,0:T(8,128)(2,1)} async-done(((bf16[2,3,64,512]{3,2,1,0:T(8,128)(2,1)}), bf16[2,3,64,512]{3,2,1,0:T(8,128)(2,1)}) %all-reduce.3.cloned.1.call-update) | async-done | bytes 393232 | tf_op jit(solution)/shard_map/psum | solution.py:116
  395.6 39.9 %while.63 = (s32[]{:T(128)}, f32[4,512,2,64]{1,0,3,2:T(4,128)}, bf16[4,512,2,64]{1,3,2,0:T(8,128)(2,1)}, bf16[2,3,64,512]{3,2,0,1:T(8,128)(2,1)}, s32[]{:T(128)}, /*index=5*/s32[]{:T(128)}) while((s32[]{:T(128)}, f32[4,512,2,64]{1,0,3,2:T(4,128)}, bf16[4,512,2,64]{1,3,2,0:T(8,128)(2,1)}, bf16[2,3,64,512]{3,2,0,1:T(8,128)(2,1)}, s32[]{:T(128)}, ...), condition=%wide.region_12.13_spmd, body=%wide.region_10.12_spmd.sunk | while | flops 204669952 | bytes 6702153 | solution.py:126
  399.8 6.1 dynamic_update_slice.19
  409.6 6.1 dynamic_update_slice.19
  419.5 6.1 dynamic_update_slice.19
  429.4 6.2 dynamic_update_slice.19
  438.2 9.5 %all-to-all-start.1 = ((bf16[8,256,128]{1,2,0:T(8,128)(2,1)}), bf16[8,256,128]{1,2,0:T(8,128)(2,1)S(1)}, u32[]{:S(2)}, u32[]{:S(2)}) async-start(bf16[8,256,128]{1,2,0:T(8,128)(2,1)} %copy.60), calls=%async_computation.1 | async-start | bytes 1048576 | tf_op jit(solution)/shard_map/all_to_all | solution.py:130
  447.7 11.2 %all-gather.15.cloned.1.call-done = bf16[1,1024,1024]{2,1,0:T(8,128)(2,1)} async-done(((bf16[1,32,1024]{2,1,0:T(8,128)(2,1)}), bf16[1,1024,1024]{2,1,0:T(8,128)(2,1)}) %all-gather.15.cloned.1.call-update) | async-done | bytes 2097168 | tf_op jit(solution)/shard_map/all_gather | solution.py:133
  461.4 89.8 %all-gather.17.cloned.1.call-done = bf16[1,3,1024,1024]{3,2,1,0:T(8,128)(2,1)} async-done(((bf16[1,3,32,1024]{3,2,1,0:T(8,128)(2,1)}), bf16[1,3,1024,1024]{3,2,1,0:T(8,128)(2,1)}) %all-gather.17.cloned.1.call-update) | async-done | bytes 6291472 | tf_op jit(solution)/shard_map/all_gather | solution.py:73
  564.0 39.1 %all-gather.6 = bf16[1,2,3,64,512]{3,1,2,0,4:T(2,128)(2,1)S(1)} all-gather(bf16[1,2,3,64,16]{3,1,2,0,4:T(2,128)(2,1)S(1)} %copy.87), channel_id=8, replica_groups=mesh['view'=32,'head'=8] {'view'}, dimensions={4}, use_global_device_ids=true | all-gather | bytes 405504 | tf_op jit(solution)/shard_map/all_gather | solution.py:104
  621.7 41.1 %while.67 = (s32[]{:T(128)}, f32[2,3,64,512]{3,2,0,1:T(8,128)S(1)}, bf16[4,512,2,64]{1,3,2,0:T(8,128)(2,1)}, s32[4,512]{1,0:T(4,128)}, bf16[4,512,2,64]{1,3,2,0:...) while((s32[]{:T(128)}, f32[2,3,64,512]{3,2,0,1:T(8,128)S(1)}, ...), condition=%wide.region_20.21_spmd.clone, body=%wide.region_19.20_spmd.clone.sunk | while | flops 415498752 | bytes 25308256 | solution.py:111
  672.6 25.1 %while.64 = (s32[]{:T(128)}, f32[4,1,512,2,64]{2,0,4,3,1:T(4,128)S(1)}, bf16[4,1,512,2,64]{2,4,3,1,0:T(8,128)(2,1)S(1)}, bf16[1,2048,2,64]{1,3,2,0:T(8,128)(2,1)...) while((s32[]{:T(128)}, f32[4,1,512,2,64]{2,0,4,3,1:T(4,128)S(1)}, ...), condition=%wide.region_18.19_spmd, body=%wide.region_16.18_spmd.sunk | while | flops 547355648 | bytes 19275860 | solution.py:100
  698.2 112.7 %all-reduce.5.cloned.1.call-done = bf16[2,3,64,512]{3,2,1,0:T(8,128)(2,1)} async-done(((bf16[2,3,64,512]{3,2,1,0:T(8,128)(2,1)}), bf16[2,3,64,512]{3,2,1,0:T(8,128)(2,1)}) %all-reduce.5.cloned.1.call-update) | async-done | bytes 393232 | tf_op jit(solution)/shard_map/psum | solution.py:116
  826.5 39.8 %while.65 = (s32[]{:T(128)}, f32[4,512,2,64]{1,0,3,2:T(4,128)}, bf16[4,512,2,64]{1,3,2,0:T(8,128)(2,1)}, bf16[2,3,64,512]{3,2,0,1:T(8,128)(2,1)}, s32[]{:T(128)}, /*index=5*/s32[]{:T(128)}) while((s32[]{:T(128)}, f32[4,512,2,64]{1,0,3,2:T(4,128)}, bf16[4,512,2,64]{1,3,2,0:T(8,128)(2,1)}, bf16[2,3,64,512]{3,2,0,1:T(8,128)(2,1)}, s32[]{:T(128)}, ...), condition=%wide.region_25.26_spmd, body=%wide.region_23.25_spmd.sunk | while | flops 204669952 | bytes 6702153 | solution.py:126
  850.2 6.1 dynamic_update_slice.21
  860.1 6.1 dynamic_update_slice.21
  868.9 9.6 %all-to-all-start.3 = ((bf16[8,256,128]{1,2,0:T(8,128)(2,1)}), bf16[8,256,128]{1,2,0:T(8,128)(2,1)S(1)}, u32[]{:S(2)}, u32[]{:S(2)}) async-start(bf16[8,256,128]{1,2,0:T(8,128)(2,1)} %copy.75), calls=%async_computation.3 | async-start | bytes 1048576 | tf_op jit(solution)/shard_map/all_to_all | solution.py:130
  878.5 10.9 %all-gather.19.cloned.1.call-done = bf16[1,1024,1024]{2,1,0:T(8,128)(2,1)} async-done(((bf16[1,32,1024]{2,1,0:T(8,128)(2,1)}), bf16[1,1024,1024]{2,1,0:T(8,128)(2,1)}) %all-gather.19.cloned.1.call-update) | async-done | bytes 2097168 | tf_op jit(solution)/shard_map/all_gather | solution.py:133
  (302 shorter events, 314.1 us)
Async XLA Ops:
  6.5 105.3 %all-gather.13.cloned.1.call-start = ((), (), s32[]{:S(2)}) async-start(), calls=%async_computation.6 | async-start | bytes 6488064 | tf_op jit(solution)/shard_map/all_gather | solution.py:73
  119.3 5.5 copy-start.13
  119.3 48.0 %all-to-all-start = ((bf16[256,3,1024]{0,1,2:T(4,128)(2,1)}), bf16[256,3,1024]{0,1,2:T(4,128)(2,1)}, u32[]{:S(2)}, u32[]{:S(2)}) async-start(bf16[256,3,1024]{0,1,2:T(4,128)(2,1)} %copy.46), calls=%async_computation | async-start | bytes 4194304 | tf_op jit(solution)/shard_map/all_to_all | solution.py:76
  124.7 41.2 %copy-start.14 = (s32[1,2048]{1,0:T(1,128)S(1)}, s32[1,2048]{1,0:T(1,128)}, u32[]{:S(2)}) copy-start(s32[1,2048]{1,0:T(1,128)} %param.21) | copy-start | bytes 24580
  124.7 255.2 %all-reduce.3.cloned.1.call-start = ((), (), s32[]{:S(2)}) async-start(), calls=%async_computation.4 | async-start | bytes 786432 | tf_op jit(solution)/shard_map/psum | solution.py:116
  164.4 2.9 copy-start.2
  231.8 28.7 %copy-start = (f32[2048,1,2,64]{0,3,2,1:T(8,128)S(1)}, f32[2048,1,2,64]{0,3,2,1:T(8,128)}, u32[]{:S(2)}) copy-start(f32[2048,1,2,64]{0,3,2,1:T(8,128)} %get-tuple-element.354) | copy-start | bytes 3145732
  232.6 226.3 %all-gather.15.cloned.1.call-start = ((), (), s32[]{:S(2)}) async-start(), calls=%async_computation.7 | async-start | bytes 2162688 | tf_op jit(solution)/shard_map/all_gather | solution.py:133
  234.2 317.0 %all-gather.17.cloned.1.call-start = ((), (), s32[]{:S(2)}) async-start(), calls=%async_computation.8 | async-start | bytes 6488064 | tf_op jit(solution)/shard_map/all_gather | solution.py:73
  262.5 2.5 copy-start.9
  269.7 2.5 copy-start.9
  276.9 2.5 copy-start.9
  284.1 2.5 copy-start.9
  437.2 21.8 %copy-start.6 = (bf16[256,1024]{1,0:T(8,128)(2,1)S(1)}, bf16[256,1024]{1,0:T(8,128)(2,1)}, u32[]{:S(2)}) copy-start(bf16[256,1024]{1,0:T(8,128)(2,1)} %param.17) | copy-start | bytes 1572868
  438.2 20.7 %all-to-all-start.1 = ((bf16[8,256,128]{1,2,0:T(8,128)(2,1)}), bf16[8,256,128]{1,2,0:T(8,128)(2,1)S(1)}, u32[]{:S(2)}, u32[]{:S(2)}) async-start(bf16[8,256,128]{1,2,0:T(8,128)(2,1)} %copy.60), calls=%async_computation.1 | async-start | bytes 1048576 | tf_op jit(solution)/shard_map/all_to_all | solution.py:130
  461.4 94.5 %copy-start.4 = (bf16[256,1024]{1,0:T(8,128)(2,1)}, bf16[256,1024]{1,0:T(8,128)(2,1)S(1)}, u32[]{:S(2)}) copy-start(bf16[256,1024]{1,0:T(8,128)(2,1)S(1)} %get-tuple-element.362) | copy-start | bytes 1572868
  558.5 5.5 copy-start.11
  558.5 45.8 %all-to-all-start.2 = ((bf16[256,3,1024]{0,1,2:T(4,128)(2,1)}), bf16[256,3,1024]{0,1,2:T(4,128)(2,1)}, u32[]{:S(2)}, u32[]{:S(2)}) async-start(bf16[256,3,1024]{0,1,2:T(4,128)(2,1)} %copy.61), calls=%async_computation.2 | async-start | bytes 4194304 | tf_op jit(solution)/shard_map/all_to_all | solution.py:76
  563.9 247.0 %all-reduce.5.cloned.1.call-start = ((), (), s32[]{:S(2)}) async-start(), calls=%async_computation.5 | async-start | bytes 786432 | tf_op jit(solution)/shard_map/psum | solution.py:116
  662.8 4.6 copy-start.1
  663.6 225.8 %all-gather.19.cloned.1.call-start = ((), (), s32[]{:S(2)}) async-start(), calls=%async_computation.9 | async-start | bytes 2162688 | tf_op jit(solution)/shard_map/all_gather | solution.py:133
  667.4 2.4 copy-start.12
  867.9 21.5 %copy-start.5 = (bf16[256,1024]{1,0:T(8,128)(2,1)S(1)}, bf16[256,1024]{1,0:T(8,128)(2,1)}, u32[]{:S(2)}) copy-start(bf16[256,1024]{1,0:T(8,128)(2,1)} %copy-done.4) | copy-start | bytes 1572868
  868.9 20.4 %all-to-all-start.3 = ((bf16[8,256,128]{1,2,0:T(8,128)(2,1)}), bf16[8,256,128]{1,2,0:T(8,128)(2,1)S(1)}, u32[]{:S(2)}, u32[]{:S(2)}) async-start(bf16[8,256,128]{1,2,0:T(8,128)(2,1)} %copy.75), calls=%async_computation.3 | async-start | bytes 1048576 | tf_op jit(solution)/shard_map/all_to_all | solution.py:130
  (4 other events, 6.6 us)
Sparse Core Ops, SparseCore 0:
  22.7 89.0 all-gather.12
  232.8 147.1 all-reduce.2
  382.9 76.0 all-gather.14
  461.7 89.4 all-gather.16
  663.7 147.1 all-reduce.4
  813.4 75.9 all-gather.18
where the time goes:
time: 915 us; the launch traced here: 900 us
  waiting for transfers between devices  397 us (43%)
  matrix products  175 us (19%)
  local copies, waits for them, and re-layouts  137 us (15%)
  blocking collectives  117 us (13%)
  starting transfers between devices  30.1 us (3%)
  other arithmetic  28.1 us (3%)
  between operations  14.6 us (2%)
    psum x2, waiting for transfers between devices, shards(): lax.psum(gradients.astype(jnp.bfloat16), 'view').astype(jnp.float32)  197 us
    all_gather x2, waiting for transfers between devices, shards(): lax.all_gather(columns, 'view', axis=1, tiled=True)  178 us
    all_gather x2, blocking collectives, shards(): full_fast = lax.all_gather(local_fast, 'view', axis=3, tiled=True)  78.1 us
    dynamic_update_slice x16, local copies, waits for them, and re-layouts, shards(): lax.map(apply_block, queries.reshape(count, block, heads_here, head_dim))  51.2 us
    all_gather x2, blocking collectives, shards(): columns = lax.all_gather(attend_weight[layer], 'head', axis=2, tiled=True)  38.4 us
    dynamic_update_slice x16, local copies, waits for them, and re-layouts, shards(): lax.map(attend_block, query_blocks)  22.5 us
    all_gather x2, waiting for transfers between devices, shards(): lax.all_gather(output_weight[layer], 'view', axis=0, tiled=True)  22.1 us
    all_to_all x2, starting transfers between devices, shards(): lax.all_to_all(mixed, 'head', split_axis=0, concat_axis=1, tiled=True)  19 us
  transfers between devices with their start and end apart: 10, of which 6 were waited for; matrix products, arithmetic and copies ran while one was open for 22% of the time, Pallas kernels for 0%

commit v1 on v0

v1 whole, which is shorter than its diff:
```python
import functools
import math

import jax
import jax.numpy as jnp
from jax import lax
from jax.experimental import pallas as pl
from jax.experimental.pallas import tpu as pltpu
from jax.sharding import PartitionSpec as P

BLOCKS = 2
NS_STEPS = 5
NEWTON = (3.4445, -4.775, 2.0315)
LEARN_RATE = 1.0
SCORE_SCALE = 0.25
EPS = 1e-05

NX, NZ, NY = 4, 8, 4
NV, NH = NX * NZ, 2 * NY

F32 = jnp.float32
BF16 = jnp.bfloat16
NT = (((1,), (1,)), ((), ()))
TN = (((0,), (0,)), ((), ()))


def dot(a, b, dims=(((1,), (0,)), ((), ())), precision=None):
    return lax.dot_general(a, b, dims, precision=precision, preferred_element_type=F32)


def low_lanes(shape):
    return lax.broadcasted_iota(jnp.int32, shape, len(shape) - 1) < 64


def head_norm(x):
    low = low_lanes(x.shape)
    sq = x * x
    first = jnp.sum(jnp.where(low, sq, 0.0), axis=-1, keepdims=True)
    second = jnp.sum(jnp.where(low, 0.0, sq), axis=-1, keepdims=True)
    return lax.rsqrt(jnp.where(low, first, second) * (1.0 / 64) + EPS)


def sigmoid(x):
    return 0.5 + 0.5 * jnp.tanh(0.5 * x)


def gray(p):
    return p + (p // 2) * (1 - 2 * (p % 2))


def start_copy(src, dst, send, recv, view, head):
    pltpu.make_async_remote_copy(
        src_ref=src,
        dst_ref=dst,
        send_sem=send,
        recv_sem=recv,
        device_id=(view, head),
        device_id_type=pl.DeviceIdType.MESH,
    ).start()


def wait_bytes(ref, sem):
    pltpu.make_async_copy(ref, ref, sem).wait()


def kernel(
    features,
    attend,
    fast,
    outw,
    mask,
    result,
    stream,
    gathered,
    qkv_w,
    fast_w,
    out_w,
    queries,
    scaled,
    keys,
    values,
    wide,
    total,
    to_sum,
    parts,
    summed,
    attended,
    to_mix,
    mixed,
    wz_recv,
    wx_recv,
    w_send,
    o_recv,
    o_send,
    og_recv,
    og_send,
    g_recv,
    g_send,
    r_recv,
    r_send,
    m_recv,
    m_send,
):
    view, head = lax.axis_index("view"), lax.axis_index("head")
    x, z = view // NZ, view % NZ
    y, core = head // 2, head % 2
    tokens = stream.shape[0]
    length = tokens * NH
    sib = y * 2 + (1 - core)
    right = ((y + 1) % NY) * 2 + core
    left = ((y + NY - 1) % NY) * 2 + core
    opposite = ((y + 2) % NY) * 2 + core
    half = tokens // 2

    def aligned(value, to):
        return pl.multiple_of(value, to)

    stream[...] = features[...]
    for b in range(BLOCKS):
        for j in range(3):
            qkv_w[b, pl.ds(aligned(view * 32, 32), 32), j * 128 : (j + 1) * 128] = attend[b, j]
        fast_w[b, :, pl.ds(aligned(view * 16, 16), 16), :] = fast[b]

    barrier = pltpu.get_barrier_semaphore()

    def greet_view(d, carry):
        pl.semaphore_signal(
            barrier, inc=1, device_id=((view + d) % NV, head), device_id_type=pl.DeviceIdType.MESH
        )
        return carry

    def greet_head(d, carry):
        pl.semaphore_signal(
            barrier, inc=1, device_id=(view, (head + d) % NH), device_id_type=pl.DeviceIdType.MESH
        )
        return carry

    lax.fori_loop(1, NV, greet_view, 0)
    lax.fori_loop(1, NH, greet_head, 0)
    pl.semaphore_wait(barrier, NV - 1 + NH - 1)

    def weights_z(b):
        own = qkv_w.at[b, pl.ds(aligned(view * 32, 32), 32)]
        own_fast = fast_w.at[b, :, pl.ds(aligned(view * 16, 16), 16)]

        def send(d, carry):
            to = x * NZ + (z + d) % NZ
            start_copy(own, own, w_send.at[b, 0], wz_recv.at[b, 0], to, head)
            return carry

        def send_fast(d, carry):
            to = x * NZ + (z + d) % NZ
            start_copy(own_fast, own_fast, w_send.at[b, 1], wz_recv.at[b, 1], to, head)
            return carry

        lax.fori_loop(1, NZ, send, 0)
        lax.fori_loop(1, NZ, send_fast, 0)

    def weights_x(b):
        wait_bytes(qkv_w.at[b, pl.ds(0, 32 * (NZ - 1))], wz_recv.at[b, 0])
        own = qkv_w.at[b, pl.ds(aligned(x * 256, 256), 256)]
        for d in (1, 3, 2):
            to = ((x + d) % NX) * NZ + z
            start_copy(own, own, w_send.at[b, 0], wx_recv.at[b, 0], to, head)
        wait_bytes(fast_w.at[b, :, pl.ds(0, 16 * (NZ - 1))], wz_recv.at[b, 1])
        own_fast = fast_w.at[b, :, pl.ds(aligned(x * 128, 128), 128)]
        for d in (1, 3, 2):
            to = ((x + d) % NX) * NZ + z
            start_copy(own_fast, own_fast, w_send.at[b, 1], wx_recv.at[b, 1], to, head)

    group = view // 4

    def output_fetch():
        rows = pl.ds(aligned(view * 32, 32), 32)
        target_group = (group - head + NH) % NH

        def send(i, carry):
            to = target_group * 4 + i

            @pl.when(to == view)
            def _():
                pltpu.make_async_copy(outw, out_w.at[:, rows], o_recv).start()

            @pl.when(to != view)
            def _():
                start_copy(outw, out_w.at[:, rows], o_send, o_recv, to, head)

            return carry

        lax.fori_loop(0, 4, send, 0)

    def output_rows(of_head):
        return pl.ds(aligned(((group + of_head) % NH) * 128, 128), 128)

    def output_share(b):
        own = out_w.at[b, output_rows(head)]
        for to in (right, left, opposite):
            start_copy(own, own, og_send.at[b], og_recv.at[b, 0], view, to)
        start_copy(own, own, og_send.at[b], og_recv.at[b, 1], view, sib)

    def output_forward(b):
        wait_bytes(out_w.at[b, pl.ds(0, 3 * 128)], og_recv.at[b, 0])
        for of_head in (right, left, opposite):
            piece = out_w.at[b, output_rows(of_head)]
            start_copy(piece, piece, og_send.at[b], og_recv.at[b, 1], view, sib)

    weights_z(0)

    def block(b, carry):
        def tokens_of(of_head, part=None):
            if part is None:
                return gathered.at[b, pl.ds(aligned(of_head * tokens, tokens), tokens)]
            return gathered.at[b, pl.ds(aligned(of_head * tokens + part * half, half), half)]

        def send_tokens(of_head, part, recv, to):
            piece = tokens_of(of_head, part)
            start_copy(piece, piece, g_send.at[b], g_recv.at[b, recv], view, to)

        for part in range(2):
            wide_rows = stream[part * half : (part + 1) * half, :].astype(F32)
            inv = lax.rsqrt(jnp.mean(wide_rows * wide_rows, axis=-1, keepdims=True) + EPS)
            gathered[b, pl.ds(aligned(head * tokens + part * half, half), half), :] = (
                wide_rows * inv
            ).astype(BF16)
        send_tokens(head, None, 6, sib)
        send_tokens(head, 0, 0, right)
        send_tokens(head, 1, 3, left)
        send_tokens(head, 1, 1, right)
        send_tokens(head, 0, 2, left)

        @pl.when(b == 0)
        def _():
            weights_z(1)
            weights_x(0)
            output_fetch()

        total[...] = jnp.zeros_like(total)
        wait_bytes(qkv_w.at[b, pl.ds(0, 256 * (NX - 1))], wx_recv.at[b, 0])
        wait_bytes(fast_w.at[b, :, pl.ds(0, 128 * (NX - 1))], wx_recv.at[b, 1])
        for j in range(3):
            weights = fast_w[b, j]
            low = low_lanes(weights.shape)
            wide[j, 0:512, :] = jnp.where(low, weights, jnp.zeros_like(weights))
            wide[j, 512:1024, :] = jnp.where(low, jnp.zeros_like(weights), weights)

        def chunk(s, carry):
            @pl.when(s == 1)
            def _():
                wait_bytes(tokens_of(sib), g_recv.at[b, 6])

            @pl.when(s == 2)
            def _():
                wait_bytes(tokens_of(left, 0), g_recv.at[b, 0])
                send_tokens(left, 0, 4, right)
                wait_bytes(tokens_of(right, 1), g_recv.at[b, 3])
                send_tokens(right, 1, 5, left)
                wait_bytes(tokens_of(right, 0), g_recv.at[b, 2])
                send_tokens(right, None, 7, sib)
                wait_bytes(tokens_of(left, 1), g_recv.at[b, 1])
                send_tokens(left, None, 8, sib)

            @pl.when(s == 3)
            def _():
                wait_bytes(tokens_of(((y + 1) % NY) * 2 + 1 - core), g_recv.at[b, 7])

            @pl.when(s == 5)
            def _():
                wait_bytes(tokens_of(((y + 3) % NY) * 2 + 1 - core), g_recv.at[b, 8])

            @pl.when(s == 6)
            def _():
                wait_bytes(tokens_of(opposite, 0), g_recv.at[b, 4])
                wait_bytes(tokens_of(opposite, 1), g_recv.at[b, 5])
                send_tokens(opposite, None, 9, sib)

            @pl.when(s == 7)
            def _():
                wait_bytes(tokens_of(((y + 2) % NY) * 2 + 1 - core), g_recv.at[b, 9])

            @pl.when(jnp.logical_and(b == 0, s == 4))
            def _():
                weights_x(1)

            source = ((y + gray(s // 2)) % NY) * 2 + (core + s % 2) % 2
            rows = pl.ds(aligned(source * tokens, tokens), tokens)
            packed = dot(gathered[b, rows, :], qkv_w[b]).astype(BF16)
            q = packed[:, 0:128].astype(F32)
            k = packed[:, 128:256].astype(F32)
            v = packed[:, 256:384]
            low = low_lanes((tokens, 128))
            q = q * head_norm(q)
            queries[rows, :] = q.astype(BF16)
            scaled[rows, :] = (q * (SCORE_SCALE * math.log2(math.e))).astype(BF16)
            k = (k * head_norm(k)).astype(BF16)
            keys[rows, :] = k
            one = jnp.ones_like(v)
            values[0, rows, :] = jnp.where(low, v, one)
            values[1, rows, :] = jnp.where(low, one, v)
            sign = -mask[:, rows].astype(F32)
            zero = jnp.zeros_like(v)
            for h in range(2):
                kh = jnp.where(low, k, zero) if h == 0 else jnp.where(low, zero, k)
                vh = jnp.where(low, v, zero) if h == 0 else jnp.where(low, zero, v)
                for part in range(2):
                    f = slice(h * 512 + part * 256, h * 512 + part * 256 + 256)
                    first = dot(wide[0, f, :], k, NT)
                    third = dot(wide[1, f, :], k, NT)
                    back = dot(wide[2, f, :], v, NT) * sign
                    sigma = sigmoid(first)
                    silu = first * sigma
                    hidden = (silu * third * sign).astype(BF16)
                    d_third = (back * silu).astype(BF16)
                    d_first = (back * third * (sigma + silu * (1.0 - sigma))).astype(BF16)
                    to = slice(part * 256, part * 256 + 256)
                    total[0, to, :] += dot(d_first, kh)
                    total[1, to, :] += dot(d_third, kh)
                    total[2, to, :] += dot(hidden, vh)
            return carry

        lax.fori_loop(0, NH, chunk, 0)

        for j in range(3):
            to_sum[j * 512 : (j + 1) * 512, :] = total[j].astype(BF16)

        def scatter(d, carry):
            to = (view + d) % NV
            start_copy(
                to_sum.at[pl.ds(aligned(to * 48, 16), 48)],
                parts.at[b, NV - 1 - d],
                r_send.at[b, 0],
                r_recv.at[b, 0],
                to,
                head,
            )
            return carry

        lax.fori_loop(1, NV, scatter, 0)

        @pl.when(b == 0)
        def _():
            wait_bytes(out_w.at[:, pl.ds(0, 128)], o_recv)

        output_share(b)

        def reduce_parts():
            wait_bytes(parts.at[b], r_recv.at[b, 0])
            mine = pl.ds(aligned(view * 48, 16), 48)

            def add(d, value):
                return value + parts[b, d].astype(F32)

            value = lax.fori_loop(0, NV - 1, add, to_sum[mine, :].astype(F32))
            summed[b, mine, :] = value.astype(BF16)

            def spread(d, carry):
                to = (view + d) % NV
                piece = summed.at[b, mine]
                start_copy(piece, piece, r_send.at[b, 1], r_recv.at[b, 1], to, head)
                return carry

            lax.fori_loop(1, NV, spread, 0)

        def attend_rows(i, carry):
            @pl.when(i == 4)
            def _():
                reduce_parts()

            rows = pl.ds(aligned(i * 256, 256), 256)
            q = scaled[rows, :]
            low = low_lanes(q.shape)
            zero = jnp.zeros_like(q)
            out = []
            for h in range(2):
                qh = jnp.where(low, q, zero) if h == 0 else jnp.where(low, zero, q)
                weighted = jnp.zeros((256, 128), F32)
                for part in range(4):
                    at = slice(part * length // 4, (part + 1) * length // 4)
                    expo = jnp.exp2(dot(qh, keys[at, :], NT)).astype(BF16)
                    weighted = weighted + dot(expo, values[h, at, :])
                out.append(weighted / pltpu.roll(weighted, 64, 1))
            attended[rows, :] = jnp.where(low_lanes(out[0].shape), out[0], out[1])
            return carry

        lax.fori_loop(0, length // 256, attend_rows, 0)
        output_forward(b)

        wait_bytes(summed.at[b, pl.ds(0, 48 * (NV - 1))], r_recv.at[b, 1])
        row = lax.broadcasted_iota(jnp.int32, (128, 128), 0)
        col = lax.broadcasted_iota(jnp.int32, (128, 128), 1)
        same = (row < 64) == (col < 64)
        eye = row == col
        exact = functools.partial(dot, precision=lax.Precision.HIGHEST)
        grams, scales = [], []
        for j in range(3):
            gradient = summed[b, j * 512 : (j + 1) * 512, :]
            gram = jnp.where(same, dot(gradient, gradient, TN), 0.0)
            diagonal = jnp.where(eye, gram, 0.0)
            squares = jnp.sum(jnp.where(same, jnp.sum(diagonal, axis=1, keepdims=True), 0.0), axis=0, keepdims=True)
            scale = lax.rsqrt(squares + 1e-06)
            scales.append(scale)
            grams.append(gram * (scale * scale))
        chains = [None] * 3
        for step in range(NS_STEPS):
            for j in range(3):
                gram = grams[j]
                poly = (
                    jnp.where(eye, NEWTON[0], 0.0)
                    + NEWTON[1] * gram
                    + NEWTON[2] * exact(gram, gram)
                )
                chains[j] = poly if step == 0 else exact(poly, chains[j])
                if step < NS_STEPS - 1:
                    grams[j] = exact(exact(poly, gram), poly)
        for j in range(3):
            gradient = summed[b, j * 512 : (j + 1) * 512, :]
            upper = chains[j].astype(BF16)
            lower = (chains[j] - upper.astype(F32)).astype(BF16)
            current = (dot(gradient, upper) + dot(gradient, lower)) * scales[j]
            updated = (fast_w[b, j].astype(F32) - LEARN_RATE * current).astype(BF16)
            low = low_lanes(updated.shape)
            wide[j, 0:512, :] = jnp.where(low, updated, jnp.zeros_like(updated))
            wide[j, 512:1024, :] = jnp.where(low, jnp.zeros_like(updated), updated)

        def apply_rows(s, carry):
            to = ((y + gray(3 - s // 2)) % NY) * 2 + (core + 1 - s % 2) % 2
            rows = pl.ds(aligned(to * tokens, tokens), tokens)
            q = queries[rows, :]
            applied = jnp.zeros((tokens, 128), F32)
            for part in range(4):
                f = slice(part * 256, part * 256 + 256)
                first = dot(q, wide[0, f, :], NT)
                third = dot(q, wide[1, f, :], NT)
                hidden = (first * sigmoid(first) * third).astype(BF16)
                applied = applied + dot(hidden, wide[2, f, :])
            to_mix[rows, :] = (attended[rows, :] + applied * head_norm(applied)).astype(BF16)
            columns = pl.ds(aligned(head * 128, 128), 128)

            @pl.when(s < NH - 1)
            def _():
                start_copy(
                    to_mix.at[rows], mixed.at[b, :, columns], m_send.at[b], m_recv.at[b], view, to
                )

            @pl.when(s == NH - 1)
            def _():
                mixed[b, :, columns] = to_mix[rows, :]

            return carry

        lax.fori_loop(0, NH, apply_rows, 0)

        wait_bytes(out_w.at[b, pl.ds(0, 4 * 128)], og_recv.at[b, 1])
        wait_bytes(mixed.at[b, :, pl.ds(0, 128 * (NH - 1))], m_recv.at[b])
        for part in range(4):
            n = slice(part * 256, part * 256 + 256)
            projected = dot(mixed[b], out_w[b, :, n])
            stream[:, n] = (stream[:, n].astype(F32) + projected).astype(BF16)

        wait_bytes(to_mix.at[pl.ds(0, tokens * (NH - 1))], m_send.at[b])
        wait_bytes(to_sum.at[pl.ds(0, 48 * (NV - 1))], r_send.at[b, 0])
        wait_bytes(summed.at[b, pl.ds(0, 48 * (NV - 1))], r_send.at[b, 1])
        wait_bytes(gathered.at[b, pl.ds(0, tokens * 7)], g_send.at[b])
        wait_bytes(out_w.at[b, pl.ds(0, 128 * 7)], og_send.at[b])
        return carry

    lax.fori_loop(0, BLOCKS, block, 0)
    result[...] = stream[...]

    for b in range(BLOCKS):
        wait_bytes(qkv_w.at[b, pl.ds(0, 32 * (NZ - 1) + 256 * (NX - 1))], w_send.at[b, 0])
        wait_bytes(fast_w.at[b, :, pl.ds(0, 16 * (NZ - 1) + 128 * (NX - 1))], w_send.at[b, 1])

    @pl.when(head == 0)
    def _():
        wait_bytes(out_w.at[:, pl.ds(0, 96)], o_send)

    @pl.when(head != 0)
    def _():
        wait_bytes(out_w.at[:, pl.ds(0, 128)], o_send)


def shards(features, attend_weight, output_weight, fast_init, update_mask):
    tokens, width = features.shape
    length = tokens * NH
    pieces = jnp.transpose(fast_init, (0, 2, 4, 1, 3)).reshape(BLOCKS, 3, 16, 128)
    vmem = pl.BlockSpec(memory_space=pltpu.VMEM)
    dma = pltpu.SemaphoreType.DMA
    return pl.pallas_call(
        kernel,
        out_shape=jax.ShapeDtypeStruct((tokens, width), BF16),
        in_specs=[vmem] * 5,
        out_specs=vmem,
        scratch_shapes=[
            pltpu.VMEM((tokens, width), BF16),
            pltpu.VMEM((BLOCKS, length, width), BF16),
            pltpu.VMEM((BLOCKS, width, 384), BF16),
            pltpu.VMEM((BLOCKS, 3, 512, 128), BF16),
            pltpu.VMEM((BLOCKS, width, width), BF16),
            pltpu.VMEM((length, 128), BF16),
            pltpu.VMEM((length, 128), BF16),
            pltpu.VMEM((length, 128), BF16),
            pltpu.VMEM((2, length, 128), BF16),
            pltpu.VMEM((3, 1024, 128), BF16),
            pltpu.VMEM((3, 512, 128), F32),
            pltpu.VMEM((1536, 128), BF16),
            pltpu.VMEM((BLOCKS, NV - 1, 48, 128), BF16),
            pltpu.VMEM((BLOCKS, 1536, 128), BF16),
            pltpu.VMEM((length, 128), F32),
            pltpu.VMEM((length, 128), BF16),
            pltpu.VMEM((BLOCKS, tokens, width), BF16),
            dma((BLOCKS, 2)),
            dma((BLOCKS, 2)),
            dma((BLOCKS, 2)),
            dma,
            dma,
            dma((BLOCKS, 2)),
            dma((BLOCKS,)),
            dma((BLOCKS, 10)),
            dma((BLOCKS,)),
            dma((BLOCKS, 2)),
            dma((BLOCKS, 2)),
            dma((BLOCKS,)),
            dma((BLOCKS,)),
        ],
        compiler_params=pltpu.CompilerParams(
            collective_id=0, has_side_effects=True, vmem_limit_bytes=56 * 1024 * 1024
        ),
        name="lact",
    )(features, attend_weight, pieces, output_weight, update_mask)


def solution(mesh):
    return jax.shard_map(
        shards,
        mesh=mesh,
        in_specs=(
            P(("view", "head"), None),
            P(None, None, "view", "head"),
            P(None, "view", None),
            P(None, "head", None, None, "view"),
            P("view", None),
        ),
        out_specs=P(("view", "head"), None),
        check_vma=False,
    )
```

time: 915 us -> 168 us (0.18); the launches traced: 900 us -> 168 us
  waiting for transfers between devices: 397 us -> 0 us
  matrix products: 175 us -> 0 us
  Pallas kernels: 0 us -> 164 us
  local copies, waits for them, and re-layouts: 137 us -> 3.41 us
  blocking collectives: 117 us -> 0 us
  starting transfers between devices: 30.1 us -> 0 us
  other arithmetic: 28.1 us -> 0 us
  between operations: 14.6 us -> 0.01 us
    all_gather x4 -> x0, waiting for transfers between devices: 200 us -> none  [the longest x2 178 us: shards(): lax.all_gather(columns, 'view', axis=1, tiled=True)]
    psum x2 -> x0, waiting for transfers between devices: 197 us -> none  [shards(): lax.psum(gradients.astype(jnp.bfloat16), 'view').astype(jnp.float32)]
    dot_general x114 -> x0, matrix products: 175 us -> none  [the longest x8 16 us: attend_block(): jnp.einsum('vqhd,vkhd->vhqk', query_block, key_views, preferred_element_t...]
    pallas_call x0 -> x1, Pallas kernels: none -> 164 us  [shards(): pl.pallas_call(kernel, out_shape=jax.ShapeDtypeStruct((tokens, width), BF...]
    all_gather x4 -> x0, blocking collectives: 117 us -> none  [the longest x2 78.1 us: shards(): full_fast = lax.all_gather(local_fast, 'view', axis=3, tiled=True)]
    dynamic_update_slice x32 -> x0, local copies, waits for them, and re-layouts: 73.7 us -> none  [the longest x16 51.2 us: shards(): lax.map(apply_block, queries.reshape(count, block, heads_here, head_dim))]
    all_to_all x4 -> x0, starting transfers between devices: 30 us -> none  [the longest x2 19 us: shards(): lax.all_to_all(mixed, 'head', split_axis=0, concat_axis=1, tiled=True)]
    convert_element_type x10 -> x0, local copies, waits for them, and re-layouts: 17.6 us -> none  [the longest x2 5.85 us: shards(): packed[:, 1].astype(jnp.float32)]
  transfers between devices with their start and end apart: 10 -> 0, of which waited for: 6 -> 0; matrix products, arithmetic and copies ran while one was open for 22% -> 0% of each run, Pallas kernels for 0% -> 0%
where the time goes in v1:
time: 168 us
  Pallas kernels  164 us (98%)
  local copies, waits for them, and re-layouts  3.41 us (2%)
    pallas_call x1, Pallas kernels, shards(): pl.pallas_call(kernel, out_shape=jax.ShapeDtypeStruct((tokens, width), BF...  164 us

profile of v1, /device:TPU:1, one launch (start us, length us, event | category | flops | bytes accessed | tf_op | source)
XLA Modules:
  0.0 167.7 jit_solution(13644658548746331137)
XLA Ops:
  0.0 0.8 copy.6
  0.8 0.7 reshape.3.fast
  1.5 164.2 %lact.1 = bf16[256,1024]{1,0:T(8,128)(2,1)} custom-call(bf16[256,1024]{1,0:T(8,128)(2,1)} %features.1, bf16[2,3,32,128]{3,2,1,0:T(8,128)(2,1)} %attend.1, bf16[2,3,16,128]{3,2,1,0:T(8,128)(2,1)} %reshape.3.fast, bf16[2,32,1024]{2,1,0:T(8,128)(2,1)} %outw.1, s32[1,2048]{1,0:T(1,128)} %mask.1), custom_call_target="tpu_custom_call" | custom-call | tf_op jit(solution)/shard_map/lact/pallas_call | solution.py:488
  165.8 1.9 %copy.8 = bf16[256,1024]{1,0:T(8,128)(2,1)} copy(bf16[256,1024]{1,0:T(8,128)(2,1)} %lact.1) | data formatting | bytes 1048576

commit v2 on v1

v2 whole, which is shorter than its diff:
```python
import math

import jax
import jax.numpy as jnp
from jax import lax
from jax.experimental import pallas as pl
from jax.experimental.pallas import tpu as pltpu
from jax.sharding import PartitionSpec as P

BLOCKS = 2
NS_STEPS = 5
NEWTON = (3.4445, -4.775, 2.0315)
LEARN_RATE = 1.0
SCORE_SCALE = 0.25
EPS = 1e-05

NX, NZ, NY = 4, 8, 4
NV, NH = NX * NZ, 2 * NY

F32 = jnp.float32
BF16 = jnp.bfloat16
NT = (((1,), (1,)), ((), ()))
TN = (((0,), (0,)), ((), ()))


def dot(a, b, dims=(((1,), (0,)), ((), ())), precision=None):
    return lax.dot_general(a, b, dims, precision=precision, preferred_element_type=F32)


def low_lanes(shape):
    return lax.broadcasted_iota(jnp.int32, shape, len(shape) - 1) < 64


def head_norm(x):
    low = low_lanes(x.shape)
    sq = x * x
    first = jnp.sum(jnp.where(low, sq, 0.0), axis=-1, keepdims=True)
    second = jnp.sum(jnp.where(low, 0.0, sq), axis=-1, keepdims=True)
    return lax.rsqrt(jnp.where(low, first, second) * (1.0 / 64) + EPS)


def split(x):
    upper = x.astype(BF16)
    return upper, (x - upper.astype(F32)).astype(BF16)


def head_norm_wide(x):
    upper, lower = split(x * x)
    row = lax.broadcasted_iota(jnp.int32, (x.shape[1], x.shape[1]), 0) // 64
    col = lax.broadcasted_iota(jnp.int32, (x.shape[1], x.shape[1]), 1) // 64
    ones = jnp.where(row == col, 1.0, 0.0).astype(BF16)
    return lax.rsqrt((dot(upper, ones) + dot(lower, ones)) * (1.0 / 64) + EPS)


def exact(a, b):
    return dot(a, b, precision=lax.Precision.HIGHEST)


def triple(a, b):
    a_upper, a_lower = split(a)
    b_upper, b_lower = split(b)
    return dot(a_upper, b_upper) + (dot(a_upper, b_lower) + dot(a_lower, b_upper))


def sigmoid(x):
    return 0.5 + 0.5 * jnp.tanh(0.5 * x)


def gray(p):
    return p + (p // 2) * (1 - 2 * (p % 2))


def start_copy(src, dst, send, recv, view, head):
    pltpu.make_async_remote_copy(
        src_ref=src,
        dst_ref=dst,
        send_sem=send,
        recv_sem=recv,
        device_id=(view, head),
        device_id_type=pl.DeviceIdType.MESH,
    ).start()


def wait_bytes(ref, sem):
    pltpu.make_async_copy(ref, ref, sem).wait()


def kernel(
    features,
    attend,
    fast,
    outw,
    mask,
    result,
    stream,
    gathered,
    qkv_w,
    fast_w,
    out_w,
    queries,
    scaled,
    keys,
    values,
    wide,
    total,
    to_sum,
    parts,
    summed,
    attended,
    to_mix,
    mixed,
    w_recv,
    w_send,
    o_recv,
    o_send,
    og_recv,
    og_send,
    g_recv,
    g_send,
    r_recv,
    r_send,
    m_recv,
    m_send,
):
    view, head = lax.axis_index("view"), lax.axis_index("head")
    x, z = view // NZ, view % NZ
    y, core = head // 2, head % 2
    tokens = stream.shape[0]
    length = tokens * NH
    sib = y * 2 + (1 - core)
    right = ((y + 1) % NY) * 2 + core
    left = ((y + NY - 1) % NY) * 2 + core
    opposite = ((y + 2) % NY) * 2 + core
    half = tokens // 2
    pair = tokens * 2

    def aligned(value, to):
        return pl.multiple_of(value, to)

    def normalize(b, part):
        rows = slice(part * half, (part + 1) * half)
        wide_rows = stream[rows, :].astype(F32)
        inv = lax.rsqrt(jnp.mean(wide_rows * wide_rows, axis=-1, keepdims=True) + EPS)
        gathered[b, pl.ds(aligned(head * tokens + part * half, half), half), :] = (
            wide_rows * inv
        ).astype(BF16)

    barrier = pltpu.get_barrier_semaphore()

    def greet(to_view, to_head):
        pl.semaphore_signal(
            barrier, inc=1, device_id=(to_view, to_head), device_id_type=pl.DeviceIdType.MESH
        )

    def greet_z(d, carry):
        greet(x * NZ + (z + d) % NZ, head)
        return carry

    for to in (right, left, sib):
        greet(view, to)
    lax.fori_loop(1, NZ, greet_z, 0)
    for d in range(1, NX):
        greet(((x + d) % NX) * NZ + z, head)
    stream[...] = features[...]
    for b in range(BLOCKS):
        for j in range(3):
            qkv_w[b, pl.ds(aligned(view * 32, 32), 32), j * 128 : (j + 1) * 128] = attend[b, j]
            fast_w[b, j, x, z] = fast[b, j]
    normalize(0, 0)
    normalize(0, 1)
    pl.semaphore_wait(barrier, 3 + NZ - 1 + NX - 1)

    def tokens_of(b, of_head, part=None):
        if part is None:
            return gathered.at[b, pl.ds(aligned(of_head * tokens, tokens), tokens)]
        return gathered.at[b, pl.ds(aligned(of_head * tokens + part * half, half), half)]

    def send_tokens(b, of_head, part, recv, to):
        piece = tokens_of(b, of_head, part)
        start_copy(piece, piece, g_send.at[b], g_recv.at[b, recv], view, to)

    def launch_tokens(b, part):
        send_tokens(b, head, part, 6, sib)
        if part == 0:
            send_tokens(b, head, 0, 0, right)
        else:
            send_tokens(b, head, 1, 3, left)
            send_tokens(b, head, 1, 1, right)
            send_tokens(b, head, 0, 2, left)

    def projections_z(b):
        own = qkv_w.at[b, pl.ds(aligned(view * 32, 32), 32)]

        def send(d, carry):
            to = x * NZ + (z + d) % NZ
            start_copy(own, own, w_send.at[b, 0], w_recv.at[b, 0], to, head)
            return carry

        lax.fori_loop(1, NZ, send, 0)

    def projections_x(b):
        wait_bytes(qkv_w.at[b, pl.ds(0, 32 * (NZ - 1))], w_recv.at[b, 0])
        own = qkv_w.at[b, pl.ds(aligned(x * 256, 256), 256)]
        for d in (1, 3, 2):
            to = ((x + d) % NX) * NZ + z
            start_copy(own, own, w_send.at[b, 1], w_recv.at[b, 1], to, head)

    def fast_x(b):
        own = fast_w.at[b, :, x, z]
        for d in (1, 3, 2):
            to = ((x + d) % NX) * NZ + z
            start_copy(own, own, w_send.at[b, 2], w_recv.at[b, 2], to, head)

    def fast_z(b):
        wait_bytes(fast_w.at[b, :, pl.ds(0, NX - 1), 0], w_recv.at[b, 2])
        own = fast_w.at[b, :, :, z]

        def send(d, carry):
            to = x * NZ + (z + d) % NZ
            start_copy(own, own, w_send.at[b, 3], w_recv.at[b, 3], to, head)
            return carry

        lax.fori_loop(1, NZ, send, 0)

    group = view // 4

    def output_fetch():
        rows = pl.ds(aligned(view * 32, 32), 32)
        target_group = (group - head + NH) % NH

        def send(i, carry):
            to = target_group * 4 + i

            @pl.when(to == view)
            def _():
                pltpu.make_async_copy(outw, out_w.at[:, rows], o_recv).start()

            @pl.when(to != view)
            def _():
                start_copy(outw, out_w.at[:, rows], o_send, o_recv, to, head)

            return carry

        lax.fori_loop(0, 4, send, 0)

    def output_rows(of_head):
        return pl.ds(aligned(((group + of_head) % NH) * 128, 128), 128)

    def output_share(b):
        own = out_w.at[b, output_rows(head)]
        for to in (right, left, opposite):
            start_copy(own, own, og_send.at[b], og_recv.at[b, 0], view, to)
        start_copy(own, own, og_send.at[b], og_recv.at[b, 1], view, sib)

    def output_forward(b):
        wait_bytes(out_w.at[b, pl.ds(0, 3 * 128)], og_recv.at[b, 0])
        for of_head in (right, left, opposite):
            piece = out_w.at[b, output_rows(of_head)]
            start_copy(piece, piece, og_send.at[b], og_recv.at[b, 1], view, sib)

    projections_z(0)
    launch_tokens(0, 0)
    launch_tokens(0, 1)
    fast_x(0)
    projections_x(0)
    fast_z(0)
    projections_z(1)
    fast_x(1)

    def block(b, carry):
        def project(s):
            @pl.when(s == 0)
            def _():
                wait_bytes(tokens_of(b, sib), g_recv.at[b, 6])
                wait_bytes(qkv_w.at[b, pl.ds(0, 256 * (NX - 1))], w_recv.at[b, 1])

                @pl.when(b == 0)
                def _():
                    output_fetch()

            @pl.when(s == 1)
            def _():
                wait_bytes(tokens_of(b, left, 0), g_recv.at[b, 0])
                send_tokens(b, left, 0, 4, right)
                wait_bytes(tokens_of(b, right, 1), g_recv.at[b, 3])
                send_tokens(b, right, 1, 5, left)
                wait_bytes(tokens_of(b, right, 0), g_recv.at[b, 2])
                send_tokens(b, right, None, 7, sib)
                wait_bytes(tokens_of(b, left, 1), g_recv.at[b, 1])
                send_tokens(b, left, None, 8, sib)

                @pl.when(b == 0)
                def _():
                    projections_x(1)
                    fast_z(1)

                wait_bytes(tokens_of(b, sib), g_recv.at[b, 7])

            @pl.when(s == 2)
            def _():
                wait_bytes(tokens_of(b, sib), g_recv.at[b, 8])

            @pl.when(s == 3)
            def _():
                wait_bytes(tokens_of(b, opposite, 0), g_recv.at[b, 4])
                wait_bytes(tokens_of(b, opposite, 1), g_recv.at[b, 5])
                send_tokens(b, opposite, None, 9, sib)
                wait_bytes(tokens_of(b, sib), g_recv.at[b, 9])

            rows = pl.ds(aligned(((y + gray(s)) % NY) * pair, pair), pair)
            packed = dot(gathered[b, rows, :], qkv_w[b]).astype(BF16)
            both = packed[:, 0:256].astype(F32)
            both = both * head_norm_wide(both)
            q = both[:, 0:128]
            v = packed[:, 256:384]
            queries[rows, :] = q.astype(BF16)
            scaled[rows, :] = (q * (SCORE_SCALE * math.log2(math.e))).astype(BF16)
            keys[rows, :] = both[:, 128:256].astype(BF16)
            low = low_lanes(v.shape)
            one = jnp.ones_like(v)
            values[0, rows, :] = jnp.where(low, v, one)
            values[1, rows, :] = jnp.where(low, one, v)

        def differentiate(s):
            @pl.when(s == 0)
            def _():
                wait_bytes(fast_w.at[b, :, :, pl.ds(0, NZ - 1)], w_recv.at[b, 3])
                total[...] = jnp.zeros_like(total)
                for j in range(3):
                    weights = fast_w[b, j].reshape(512, 128)
                    low = low_lanes(weights.shape)
                    wide[j, 0:512, :] = jnp.where(low, weights, jnp.zeros_like(weights))
                    wide[j, 512:1024, :] = jnp.where(low, jnp.zeros_like(weights), weights)

            rows = pl.ds(aligned(((y + gray(s)) % NY) * pair, pair), pair)
            k = keys[rows, :]
            low = low_lanes(k.shape)
            zero = jnp.zeros_like(k)
            sign = -mask[:, rows].astype(F32)
            for h in range(2):
                v = values[h, rows, :]
                kh = jnp.where(low, k, zero) if h == 0 else jnp.where(low, zero, k)
                vh = jnp.where(low, v, zero) if h == 0 else jnp.where(low, zero, v)
                f = slice(h * 512, h * 512 + 512)
                first = dot(wide[0, f, :], k, NT)
                third = dot(wide[1, f, :], k, NT)
                back = dot(wide[2, f, :], v, NT) * sign
                sigma = sigmoid(first)
                silu = first * sigma
                hidden = (silu * third * sign).astype(BF16)
                d_third = (back * silu).astype(BF16)
                d_first = (back * third * (sigma + silu * (1.0 - sigma))).astype(BF16)
                total[0] += dot(d_first, kh)
                total[1] += dot(d_third, kh)
                total[2] += dot(hidden, vh)

        def turn(u, carry):
            s = b * (u // 2) + (1 - b) * (u % 4)
            kind = b * (u % 2) + (1 - b) * (u // 4)

            @pl.when(kind == 0)
            def _():
                project(s)

            @pl.when(kind == 1)
            def _():
                differentiate(s)

            return carry

        lax.fori_loop(0, 2 * NY, turn, 0)

        for j in range(3):
            to_sum[j * 512 : (j + 1) * 512, :] = total[j].astype(BF16)

        def scatter(d, carry):
            to = (view + d) % NV
            start_copy(
                to_sum.at[pl.ds(aligned(to * 48, 16), 48)],
                parts.at[b, NV - 1 - d],
                r_send.at[b, 0],
                r_recv.at[b, 0],
                to,
                head,
            )
            return carry

        lax.fori_loop(1, NV, scatter, 0)

        @pl.when(b == 0)
        def _():
            wait_bytes(out_w.at[:, pl.ds(0, 128)], o_recv)

        output_share(b)

        def reduce_parts():
            wait_bytes(parts.at[b], r_recv.at[b, 0])
            mine = pl.ds(aligned(view * 48, 16), 48)

            value = to_sum[mine, :].astype(F32) + jnp.sum(parts[b].astype(F32), axis=0)
            summed[b, mine, :] = value.astype(BF16)

            def spread(d, carry):
                to = (view + d) % NV
                piece = summed.at[b, mine]
                start_copy(piece, piece, r_send.at[b, 1], r_recv.at[b, 1], to, head)
                return carry

            lax.fori_loop(1, NV, spread, 0)

        def attend_rows(i, carry):
            @pl.when(i == 1)
            def _():
                reduce_parts()

            rows = pl.ds(aligned(i * 1024, 1024), 1024)
            q = scaled[rows, :]
            low = low_lanes(q.shape)
            zero = jnp.zeros_like(q)
            own = [jnp.where(low, q, zero), jnp.where(low, zero, q)]
            weighted = [jnp.zeros(q.shape, F32)] * 2
            for part in range(length // 256):
                at = slice(part * 256, (part + 1) * 256)
                for h in range(2):
                    expo = jnp.exp2(dot(own[h], keys[at, :], NT)).astype(BF16)
                    weighted[h] = weighted[h] + dot(expo, values[h, at, :])
            out = [each / pltpu.roll(each, 64, 1) for each in weighted]
            attended[rows, :] = jnp.where(low_lanes(out[0].shape), out[0], out[1])
            return carry

        lax.fori_loop(0, length // 1024, attend_rows, 0)
        output_forward(b)

        wait_bytes(summed.at[b, pl.ds(0, 48 * (NV - 1))], r_recv.at[b, 1])
        row = lax.broadcasted_iota(jnp.int32, (128, 128), 0)
        col = lax.broadcasted_iota(jnp.int32, (128, 128), 1)
        same = (row < 64) == (col < 64)
        eye = row == col
        grams, scales = [], []
        for j in range(3):
            gradient = summed[b, j * 512 : (j + 1) * 512, :]
            gram = jnp.where(same, dot(gradient, gradient, TN), 0.0)
            diagonal = jnp.where(eye, gram, 0.0)
            squares = jnp.sum(jnp.where(same, jnp.sum(diagonal, axis=1, keepdims=True), 0.0), axis=0, keepdims=True)
            scale = lax.rsqrt(squares + 1e-06)
            scales.append(scale)
            grams.append(gram * (scale * scale))
        for step in range(NS_STEPS):
            product = exact if step < 2 else triple
            polys = [
                jnp.where(eye, NEWTON[0], 0.0)
                + NEWTON[1] * gram
                + NEWTON[2] * product(gram, gram)
                for gram in grams
            ]
            if step < NS_STEPS - 1:
                halves = [product(poly, gram) for poly, gram in zip(polys, grams)]
                grams = [product(each, poly) for each, poly in zip(halves, polys)]
            if step == 0:
                chains = polys
            else:
                chains = [triple(poly, chain) for poly, chain in zip(polys, chains)]
        for j in range(3):
            gradient = summed[b, j * 512 : (j + 1) * 512, :]
            upper, lower = split(chains[j])
            current = (dot(gradient, upper) + dot(gradient, lower)) * scales[j]
            updated = (fast_w[b, j].reshape(512, 128).astype(F32) - LEARN_RATE * current).astype(BF16)
            low = low_lanes(updated.shape)
            wide[j, 0:512, :] = jnp.where(low, updated, jnp.zeros_like(updated))
            wide[j, 512:1024, :] = jnp.where(low, jnp.zeros_like(updated), updated)

        def apply_rows(s, carry):
            chip = (y + gray(NY - 1 - s)) % NY
            rows = pl.ds(aligned(chip * pair, pair), pair)
            q = queries[rows, :]
            applied = jnp.zeros((pair, 128), F32)
            for part in range(4):
                f = slice(part * 256, part * 256 + 256)
                first = dot(q, wide[0, f, :], NT)
                third = dot(q, wide[1, f, :], NT)
                hidden = (first * sigmoid(first) * third).astype(BF16)
                applied = applied + dot(hidden, wide[2, f, :])
            to_mix[rows, :] = (attended[rows, :] + applied * head_norm(applied)).astype(BF16)
            columns = pl.ds(aligned(head * 128, 128), 128)

            def home(to):
                mine = to_mix.at[pl.ds(aligned(to * tokens, tokens), tokens)]
                start_copy(mine, mixed.at[b, :, columns], m_send.at[b], m_recv.at[b], view, to)

            home(chip * 2 + 1 - core)

            @pl.when(s < NY - 1)
            def _():
                home(chip * 2 + core)

            @pl.when(s == NY - 1)
            def _():
                mixed[b, :, columns] = to_mix[pl.ds(aligned(head * tokens, tokens), tokens), :]

            return carry

        lax.fori_loop(0, NY, apply_rows, 0)

        wait_bytes(out_w.at[b, pl.ds(0, 4 * 128)], og_recv.at[b, 1])
        wait_bytes(mixed.at[b, :, pl.ds(0, 128 * (NH - 1))], m_recv.at[b])
        for part in range(2):
            rows = slice(part * half, (part + 1) * half)
            projected = dot(mixed[b, rows, :], out_w[b])
            stream[rows, :] = (stream[rows, :].astype(F32) + projected).astype(BF16)

            @pl.when(b < BLOCKS - 1)
            def _():
                normalize(b + 1, part)
                launch_tokens(b + 1, part)

        wait_bytes(to_mix.at[pl.ds(0, tokens * (NH - 1))], m_send.at[b])
        wait_bytes(to_sum.at[pl.ds(0, 48 * (NV - 1))], r_send.at[b, 0])
        wait_bytes(summed.at[b, pl.ds(0, 48 * (NV - 1))], r_send.at[b, 1])
        wait_bytes(gathered.at[b, pl.ds(0, tokens * 7)], g_send.at[b])
        wait_bytes(out_w.at[b, pl.ds(0, 128 * 7)], og_send.at[b])
        return carry

    lax.fori_loop(0, BLOCKS, block, 0)
    result[...] = stream[...]

    for b in range(BLOCKS):
        wait_bytes(qkv_w.at[b, pl.ds(0, 32 * (NZ - 1))], w_send.at[b, 0])
        wait_bytes(qkv_w.at[b, pl.ds(0, 256 * (NX - 1))], w_send.at[b, 1])
        wait_bytes(fast_w.at[b, :, pl.ds(0, NX - 1), 0], w_send.at[b, 2])
        wait_bytes(fast_w.at[b, :, :, pl.ds(0, NZ - 1)], w_send.at[b, 3])

    @pl.when(head == 0)
    def _():
        wait_bytes(out_w.at[:, pl.ds(0, 96)], o_send)

    @pl.when(head != 0)
    def _():
        wait_bytes(out_w.at[:, pl.ds(0, 128)], o_send)


def shards(features, attend_weight, output_weight, fast_init, update_mask):
    tokens, width = features.shape
    length = tokens * NH
    pieces = jnp.transpose(fast_init, (0, 2, 4, 1, 3)).reshape(BLOCKS, 3, 16, 128)
    vmem = pl.BlockSpec(memory_space=pltpu.VMEM)
    dma = pltpu.SemaphoreType.DMA
    return pl.pallas_call(
        kernel,
        out_shape=jax.ShapeDtypeStruct((tokens, width), BF16),
        in_specs=[vmem] * 5,
        out_specs=vmem,
        scratch_shapes=[
            pltpu.VMEM((tokens, width), BF16),
            pltpu.VMEM((BLOCKS, length, width), BF16),
            pltpu.VMEM((BLOCKS, width, 384), BF16),
            pltpu.VMEM((BLOCKS, 3, NX, NZ, 16, 128), BF16),
            pltpu.VMEM((BLOCKS, width, width), BF16),
            pltpu.VMEM((length, 128), BF16),
            pltpu.VMEM((length, 128), BF16),
            pltpu.VMEM((length, 128), BF16),
            pltpu.VMEM((2, length, 128), BF16),
            pltpu.VMEM((3, 1024, 128), BF16),
            pltpu.VMEM((3, 512, 128), F32),
            pltpu.VMEM((1536, 128), BF16),
            pltpu.VMEM((BLOCKS, NV - 1, 48, 128), BF16),
            pltpu.VMEM((BLOCKS, 1536, 128), BF16),
            pltpu.VMEM((length, 128), F32),
            pltpu.VMEM((length, 128), BF16),
            pltpu.VMEM((BLOCKS, tokens, width), BF16),
            dma((BLOCKS, 4)),
            dma((BLOCKS, 4)),
            dma,
            dma,
            dma((BLOCKS, 2)),
            dma((BLOCKS,)),
            dma((BLOCKS, 10)),
            dma((BLOCKS,)),
            dma((BLOCKS, 2)),
            dma((BLOCKS, 2)),
            dma((BLOCKS,)),
            dma((BLOCKS,)),
        ],
        compiler_params=pltpu.CompilerParams(
            collective_id=0, has_side_effects=True, vmem_limit_bytes=56 * 1024 * 1024
        ),
        name="lact",
    )(features, attend_weight, pieces, output_weight, update_mask)


def solution(mesh):
    return jax.shard_map(
        shards,
        mesh=mesh,
        in_specs=(
            P(("view", "head"), None),
            P(None, None, "view", "head"),
            P(None, "view", None),
            P(None, "head", None, None, "view"),
            P("view", None),
        ),
        out_specs=P(("view", "head"), None),
        check_vma=False,
    )
```

time: 168 us -> 152 us (0.905)
  Pallas kernels: 164 us -> 148 us
    pallas_call x1, Pallas kernels: 164 us -> 148 us  [shards(): pl.pallas_call(kernel, out_shape=jax.ShapeDtypeStruct((tokens, width), BF...]
where the time goes in v2:
time: 152 us; the launch traced here: 151 us
  Pallas kernels  148 us (97%)
  local copies, waits for them, and re-layouts  3.41 us (2%)
    pallas_call x1, Pallas kernels, shards(): pl.pallas_call(kernel, out_shape=jax.ShapeDtypeStruct((tokens, width), BF...  148 us

profile of v2, /device:TPU:1, one launch (start us, length us, event | category | flops | bytes accessed | tf_op | source)
XLA Modules:
  0.0 151.4 jit_solution(3376954584844935736)
XLA Ops:
  0.0 0.8 copy.6
  0.8 0.7 reshape.3.fast
  1.5 148.0 %lact.1 = bf16[256,1024]{1,0:T(8,128)(2,1)} custom-call(bf16[256,1024]{1,0:T(8,128)(2,1)} %features.1, bf16[2,3,32,128]{3,2,1,0:T(8,128)(2,1)} %attend.1, bf16[2,3,16,128]{3,2,1,0:T(8,128)(2,1)} %reshape.3.fast, bf16[2,32,1024]{2,1,0:T(8,128)(2,1)} %outw.1, s32[1,2048]{1,0:T(1,128)} %mask.1), custom_call_target="tpu_custom_call" | custom-call | tf_op jit(solution)/shard_map/lact/pallas_call | solution.py:547
  149.5 1.9 %copy.8 = bf16[256,1024]{1,0:T(8,128)(2,1)} copy(bf16[256,1024]{1,0:T(8,128)(2,1)} %lact.1) | data formatting | bytes 1048576

commit v3 on v2

--- a/solution.py
+++ b/solution.py
@@ -16,6 +16,8 @@
 
 NX, NZ, NY = 4, 8, 4
 NV, NH = NX * NZ, 2 * NY
+
+COLUMNS = (slice(0, 128), slice(128, 384))
 
 F32 = jnp.float32
 BF16 = jnp.bfloat16
@@ -175,49 +177,51 @@
             return gathered.at[b, pl.ds(aligned(of_head * tokens, tokens), tokens)]
         return gathered.at[b, pl.ds(aligned(of_head * tokens + part * half, half), half)]
 
-    def send_tokens(b, of_head, part, recv, to):
+    def send_tokens(b, of_head, part, recv, to, columns=None):
         piece = tokens_of(b, of_head, part)
+        if columns is not None:
+            piece = piece.at[:, columns]
         start_copy(piece, piece, g_send.at[b], g_recv.at[b, recv], view, to)
 
     def launch_tokens(b, part):
-        send_tokens(b, head, part, 6, sib)
-        if part == 0:
-            send_tokens(b, head, 0, 0, right)
-        else:
-            send_tokens(b, head, 1, 3, left)
-            send_tokens(b, head, 1, 1, right)
-            send_tokens(b, head, 0, 2, left)
+        send_tokens(b, head, part, part, right)
+        send_tokens(b, head, part, 2 + part, left)
+        send_tokens(b, head, part, 4, sib)
 
     def projections_z(b):
-        own = qkv_w.at[b, pl.ds(aligned(view * 32, 32), 32)]
-
-        def send(d, carry):
-            to = x * NZ + (z + d) % NZ
-            start_copy(own, own, w_send.at[b, 0], w_recv.at[b, 0], to, head)
-            return carry
-
-        lax.fori_loop(1, NZ, send, 0)
+        rows = pl.ds(aligned(view * 32, 32), 32)
+        for part, columns in enumerate(COLUMNS):
+            own = qkv_w.at[b, rows, columns]
+
+            def send(d, carry):
+                to = x * NZ + (z + d) % NZ
+                start_copy(own, own, w_send.at[b, part], w_recv.at[b, part], to, head)
+                return carry
+
+            lax.fori_loop(1, NZ, send, 0)
 
     def projections_x(b):
-        wait_bytes(qkv_w.at[b, pl.ds(0, 32 * (NZ - 1))], w_recv.at[b, 0])
-        own = qkv_w.at[b, pl.ds(aligned(x * 256, 256), 256)]
-        for d in (1, 3, 2):
-            to = ((x + d) % NX) * NZ + z
-            start_copy(own, own, w_send.at[b, 1], w_recv.at[b, 1], to, head)
+        rows = pl.ds(aligned(x * 256, 256), 256)
+        for part, columns in enumerate(COLUMNS):
+            wait_bytes(qkv_w.at[b, pl.ds(0, 32 * (NZ - 1)), columns], w_recv.at[b, part])
+            own = qkv_w.at[b, rows, columns]
+            for d in (1, 3, 2):
+                to = ((x + d) % NX) * NZ + z
+                start_copy(own, own, w_send.at[b, 2 + part], w_recv.at[b, 2 + part], to, head)
 
     def fast_x(b):
         own = fast_w.at[b, :, x, z]
         for d in (1, 3, 2):
             to = ((x + d) % NX) * NZ + z
-            start_copy(own, own, w_send.at[b, 2], w_recv.at[b, 2], to, head)
+            start_copy(own, own, w_send.at[b, 4], w_recv.at[b, 4], to, head)
 
     def fast_z(b):
-        wait_bytes(fast_w.at[b, :, pl.ds(0, NX - 1), 0], w_recv.at[b, 2])
+        wait_bytes(fast_w.at[b, :, pl.ds(0, NX - 1), 0], w_recv.at[b, 4])
         own = fast_w.at[b, :, :, z]
 
         def send(d, carry):
             to = x * NZ + (z + d) % NZ
-            start_copy(own, own, w_send.at[b, 3], w_recv.at[b, 3], to, head)
+            start_copy(own, own, w_send.at[b, 5], w_recv.at[b, 5], to, head)
             return carry
 
         lax.fori_loop(1, NZ, send, 0)
@@ -264,15 +268,14 @@
     fast_x(0)
     projections_x(0)
     fast_z(0)
-    projections_z(1)
-    fast_x(1)
 
     def block(b, carry):
         def project(s):
             @pl.when(s == 0)
             def _():
-                wait_bytes(tokens_of(b, sib), g_recv.at[b, 6])
-                wait_bytes(qkv_w.at[b, pl.ds(0, 256 * (NX - 1))], w_recv.at[b, 1])
+                wait_bytes(tokens_of(b, sib), g_recv.at[b, 4])
+                for part, columns in enumerate(COLUMNS):
+                    wait_bytes(qkv_w.at[b, pl.ds(0, 256 * (NX - 1)), columns], w_recv.at[b, 2 + part])
 
                 @pl.when(b == 0)
                 def _():
@@ -280,32 +283,26 @@
 
             @pl.when(s == 1)
             def _():
-                wait_bytes(tokens_of(b, left, 0), g_recv.at[b, 0])
-                send_tokens(b, left, 0, 4, right)
-                wait_bytes(tokens_of(b, right, 1), g_recv.at[b, 3])
-                send_tokens(b, right, 1, 5, left)
-                wait_bytes(tokens_of(b, right, 0), g_recv.at[b, 2])
-                send_tokens(b, right, None, 7, sib)
-                wait_bytes(tokens_of(b, left, 1), g_recv.at[b, 1])
-                send_tokens(b, left, None, 8, sib)
-
-                @pl.when(b == 0)
-                def _():
-                    projections_x(1)
-                    fast_z(1)
-
-                wait_bytes(tokens_of(b, sib), g_recv.at[b, 7])
+                for part in range(2):
+                    wait_bytes(tokens_of(b, left, part), g_recv.at[b, part])
+                    send_tokens(b, left, part, 7 + part, right, slice(0, 512))
+                    wait_bytes(tokens_of(b, right, part), g_recv.at[b, 2 + part])
+                    send_tokens(b, right, part, 9 + part, left, slice(512, 1024))
+                    send_tokens(b, right, part, 5, sib)
+                    send_tokens(b, left, part, 6, sib)
+                wait_bytes(tokens_of(b, sib), g_recv.at[b, 5])
 
             @pl.when(s == 2)
             def _():
-                wait_bytes(tokens_of(b, sib), g_recv.at[b, 8])
+                wait_bytes(tokens_of(b, sib), g_recv.at[b, 6])
 
             @pl.when(s == 3)
             def _():
-                wait_bytes(tokens_of(b, opposite, 0), g_recv.at[b, 4])
-                wait_bytes(tokens_of(b, opposite, 1), g_recv.at[b, 5])
-                send_tokens(b, opposite, None, 9, sib)
-                wait_bytes(tokens_of(b, sib), g_recv.at[b, 9])
+                for part in range(2):
+                    wait_bytes(tokens_of(b, opposite, part).at[:, 0:512], g_recv.at[b, 7 + part])
+                    wait_bytes(tokens_of(b, opposite, part).at[:, 512:1024], g_recv.at[b, 9 + part])
+                    send_tokens(b, opposite, part, 11, sib)
+                wait_bytes(tokens_of(b, sib), g_recv.at[b, 11])
 
             rows = pl.ds(aligned(((y + gray(s)) % NY) * pair, pair), pair)
             packed = dot(gathered[b, rows, :], qkv_w[b]).astype(BF16)
@@ -324,7 +321,13 @@
         def differentiate(s):
             @pl.when(s == 0)
             def _():
-                wait_bytes(fast_w.at[b, :, :, pl.ds(0, NZ - 1)], w_recv.at[b, 3])
+                wait_bytes(fast_w.at[b, :, :, pl.ds(0, NZ - 1)], w_recv.at[b, 5])
+
+                @pl.when(b == 0)
+                def _():
+                    projections_z(1)
+                    fast_x(1)
+
                 total[...] = jnp.zeros_like(total)
                 for j in range(3):
                     weights = fast_w[b, j].reshape(512, 128)
@@ -432,6 +435,12 @@
         output_forward(b)
 
         wait_bytes(summed.at[b, pl.ds(0, 48 * (NV - 1))], r_recv.at[b, 1])
+
+        @pl.when(b == 0)
+        def _():
+            projections_x(1)
+            fast_z(1)
+
         row = lax.broadcasted_iota(jnp.int32, (128, 128), 0)
         col = lax.broadcasted_iota(jnp.int32, (128, 128), 1)
         same = (row < 64) == (col < 64)
@@ -469,42 +478,44 @@
             wide[j, 0:512, :] = jnp.where(low, updated, jnp.zeros_like(updated))
             wide[j, 512:1024, :] = jnp.where(low, jnp.zeros_like(updated), updated)
 
-        def apply_rows(s, carry):
+        def apply_rows(u, carry):
+            part, s = u // NY, u % NY
             chip = (y + gray(NY - 1 - s)) % NY
-            rows = pl.ds(aligned(chip * pair, pair), pair)
-            q = queries[rows, :]
-            applied = jnp.zeros((pair, 128), F32)
-            for part in range(4):
-                f = slice(part * 256, part * 256 + 256)
+            near = pl.ds(aligned((chip * 2 + core) * tokens + part * half, half), half)
+            far = pl.ds(aligned((chip * 2 + 1 - core) * tokens + part * half, half), half)
+            q = jnp.concatenate([queries[far, :], queries[near, :]], axis=0)
+            applied = jnp.zeros(q.shape, F32)
+            for block_f in range(2):
+                f = slice(block_f * 512, block_f * 512 + 512)
                 first = dot(q, wide[0, f, :], NT)
                 third = dot(q, wide[1, f, :], NT)
                 hidden = (first * sigmoid(first) * third).astype(BF16)
                 applied = applied + dot(hidden, wide[2, f, :])
-            to_mix[rows, :] = (attended[rows, :] + applied * head_norm(applied)).astype(BF16)
-            columns = pl.ds(aligned(head * 128, 128), 128)
-
-            def home(to):
-                mine = to_mix.at[pl.ds(aligned(to * tokens, tokens), tokens)]
-                start_copy(mine, mixed.at[b, :, columns], m_send.at[b], m_recv.at[b], view, to)
-
-            home(chip * 2 + 1 - core)
+            applied = applied * head_norm(applied)
+            to_mix[far, :] = (attended[far, :] + applied[0:half]).astype(BF16)
+            to_mix[near, :] = (attended[near, :] + applied[half:]).astype(BF16)
+            target = mixed.at[
+                b, pl.ds(aligned(part * half, half), half), pl.ds(aligned(head * 128, 128), 128)
+            ]
+            sems = m_send.at[b], m_recv.at[b, part]
+            start_copy(to_mix.at[far], target, *sems, view, chip * 2 + 1 - core)
 
             @pl.when(s < NY - 1)
             def _():
-                home(chip * 2 + core)
+                start_copy(to_mix.at[near], target, *sems, view, chip * 2 + core)
 
             @pl.when(s == NY - 1)
             def _():
-                mixed[b, :, columns] = to_mix[pl.ds(aligned(head * tokens, tokens), tokens), :]
+                target[...] = to_mix[near, :]
 
             return carry
 
-        lax.fori_loop(0, NY, apply_rows, 0)
+        lax.fori_loop(0, 2 * NY, apply_rows, 0)
 
         wait_bytes(out_w.at[b, pl.ds(0, 4 * 128)], og_recv.at[b, 1])
-        wait_bytes(mixed.at[b, :, pl.ds(0, 128 * (NH - 1))], m_recv.at[b])
         for part in range(2):
             rows = slice(part * half, (part + 1) * half)
+            wait_bytes(mixed.at[b, rows, pl.ds(0, 128 * (NH - 1))], m_recv.at[b, part])
             projected = dot(mixed[b, rows, :], out_w[b])
             stream[rows, :] = (stream[rows, :].astype(F32) + projected).astype(BF16)
 
@@ -524,10 +535,11 @@
     result[...] = stream[...]
 
     for b in range(BLOCKS):
-        wait_bytes(qkv_w.at[b, pl.ds(0, 32 * (NZ - 1))], w_send.at[b, 0])
-        wait_bytes(qkv_w.at[b, pl.ds(0, 256 * (NX - 1))], w_send.at[b, 1])
-        wait_bytes(fast_w.at[b, :, pl.ds(0, NX - 1), 0], w_send.at[b, 2])
-        wait_bytes(fast_w.at[b, :, :, pl.ds(0, NZ - 1)], w_send.at[b, 3])
+        for part, columns in enumerate(COLUMNS):
+            wait_bytes(qkv_w.at[b, pl.ds(0, 32 * (NZ - 1)), columns], w_send.at[b, part])
+            wait_bytes(qkv_w.at[b, pl.ds(0, 256 * (NX - 1)), columns], w_send.at[b, 2 + part])
+        wait_bytes(fast_w.at[b, :, pl.ds(0, NX - 1), 0], w_send.at[b, 4])
+        wait_bytes(fast_w.at[b, :, :, pl.ds(0, NZ - 1)], w_send.at[b, 5])
 
     @pl.when(head == 0)
     def _():
@@ -567,17 +579,17 @@
             pltpu.VMEM((length, 128), F32),
             pltpu.VMEM((length, 128), BF16),
             pltpu.VMEM((BLOCKS, tokens, width), BF16),
-            dma((BLOCKS, 4)),
-            dma((BLOCKS, 4)),
+            dma((BLOCKS, 6)),
+            dma((BLOCKS, 6)),
             dma,
             dma,
             dma((BLOCKS, 2)),
             dma((BLOCKS,)),
-            dma((BLOCKS, 10)),
+            dma((BLOCKS, 12)),
             dma((BLOCKS,)),
             dma((BLOCKS, 2)),
             dma((BLOCKS, 2)),
-            dma((BLOCKS,)),
+            dma((BLOCKS, 2)),
             dma((BLOCKS,)),
         ],
         compiler_params=pltpu.CompilerParams(

time: 152 us -> 146 us (0.961)
  Pallas kernels: 148 us -> 142 us
    pallas_call x1, Pallas kernels: 148 us -> 142 us  [shards(): pl.pallas_call(kernel, out_shape=jax.ShapeDtypeStruct((tokens, width), BF...]
where the time goes in v3:
time: 146 us; the launch traced here: 145 us
  Pallas kernels  142 us (97%)
  local copies, waits for them, and re-layouts  3.41 us (2%)
    pallas_call x1, Pallas kernels, shards(): pl.pallas_call(kernel, out_shape=jax.ShapeDtypeStruct((tokens, width), BF...  142 us

profile of v3, /device:TPU:1, one launch (start us, length us, event | category | flops | bytes accessed | tf_op | source)
XLA Modules:
  0.0 145.5 jit_solution(18284466361853910861)
XLA Ops:
  0.0 0.8 copy.6
  0.8 0.7 reshape.3.fast
  1.5 142.0 %lact.1 = bf16[256,1024]{1,0:T(8,128)(2,1)} custom-call(bf16[256,1024]{1,0:T(8,128)(2,1)} %features.1, bf16[2,3,32,128]{3,2,1,0:T(8,128)(2,1)} %attend.1, bf16[2,3,16,128]{3,2,1,0:T(8,128)(2,1)} %reshape.3.fast, bf16[2,32,1024]{2,1,0:T(8,128)(2,1)} %outw.1, s32[1,2048]{1,0:T(1,128)} %mask.1), custom_call_target="tpu_custom_call" | custom-call | tf_op jit(solution)/shard_map/lact/pallas_call | solution.py:559
  143.6 1.9 %copy.8 = bf16[256,1024]{1,0:T(8,128)(2,1)} copy(bf16[256,1024]{1,0:T(8,128)(2,1)} %lact.1) | data formatting | bytes 1048576

commit v4 on v3

--- a/solution.py
+++ b/solution.py
@@ -106,7 +106,11 @@
     wide,
     total,
     to_sum,
-    parts,
+    a_x,
+    c_z,
+    a_z,
+    c_x,
+    middle,
     summed,
     attended,
     to_mix,
@@ -167,7 +171,7 @@
     for b in range(BLOCKS):
         for j in range(3):
             qkv_w[b, pl.ds(aligned(view * 32, 32), 32), j * 128 : (j + 1) * 128] = attend[b, j]
-            fast_w[b, j, x, z] = fast[b, j]
+            fast_w[b, j, x, z] = jnp.concatenate([fast[b, 0, j], fast[b, 1, j]], axis=1)
     normalize(0, 0)
     normalize(0, 1)
     pl.semaphore_wait(barrier, 3 + NZ - 1 + NX - 1)
@@ -358,8 +362,9 @@
                 total[2] += dot(hidden, vh)
 
         def turn(u, carry):
-            s = b * (u // 2) + (1 - b) * (u % 4)
-            kind = b * (u % 2) + (1 - b) * (u // 4)
+            late = b + (1 - b) * (u // 4)
+            s = late * (u // 2) + (1 - late) * (u % 2)
+            kind = late * (u % 2) + (1 - late) * (u // 2)
 
             @pl.when(kind == 0)
             def _():
@@ -376,19 +381,31 @@
         for j in range(3):
             to_sum[j * 512 : (j + 1) * 512, :] = total[j].astype(BF16)
 
-        def scatter(d, carry):
-            to = (view + d) % NV
-            start_copy(
-                to_sum.at[pl.ds(aligned(to * 48, 16), 48)],
-                parts.at[b, NV - 1 - d],
-                r_send.at[b, 0],
-                r_recv.at[b, 0],
-                to,
-                head,
-            )
-            return carry
-
-        lax.fori_loop(1, NV, scatter, 0)
+        def along_x(source, target, sem):
+            for d in (1, 3, 2):
+                to = (x + d) % NX
+                start_copy(
+                    source(to), target(d - 1), r_send.at[b, sem], r_recv.at[b, sem], to * NZ + z, head
+                )
+
+        def along_z(source, target, sem):
+            def send(d, carry):
+                to = (z + d) % NZ
+                start_copy(
+                    source(to), target(d - 1), r_send.at[b, sem], r_recv.at[b, sem], x * NZ + to, head
+                )
+                return carry
+
+            lax.fori_loop(1, NZ, send, 0)
+
+        def rows_of(ref, start, count):
+            return ref.at[pl.ds(aligned(start, 16), count)]
+
+        def add(own, slots):
+            return own.astype(F32) + jnp.sum(slots.astype(F32), axis=0)
+
+        along_x(lambda to: rows_of(to_sum, to * 256, 256), lambda i: a_x.at[b, i], 0)
+        along_z(lambda to: rows_of(to_sum, 1024 + to * 64, 64), lambda i: c_z.at[b, i], 1)
 
         @pl.when(b == 0)
         def _():
@@ -397,19 +414,34 @@
         output_share(b)
 
         def reduce_parts():
-            wait_bytes(parts.at[b], r_recv.at[b, 0])
-            mine = pl.ds(aligned(view * 48, 16), 48)
-
-            value = to_sum[mine, :].astype(F32) + jnp.sum(parts[b].astype(F32), axis=0)
-            summed[b, mine, :] = value.astype(BF16)
-
-            def spread(d, carry):
-                to = (view + d) % NV
-                piece = summed.at[b, mine]
-                start_copy(piece, piece, r_send.at[b, 1], r_recv.at[b, 1], to, head)
-                return carry
-
-            lax.fori_loop(1, NV, spread, 0)
+            wait_bytes(a_x.at[b], r_recv.at[b, 0])
+            own = to_sum[pl.ds(aligned(x * 256, 16), 256), :]
+            middle[0:256, :] = add(own, a_x[b]).astype(BF16)
+            along_z(lambda to: rows_of(middle, to * 32, 32), lambda i: a_z.at[b, i], 2)
+            wait_bytes(c_z.at[b], r_recv.at[b, 1])
+            own = to_sum[pl.ds(aligned(1024 + z * 64, 16), 64), :]
+            middle[256:320, :] = add(own, c_z[b]).astype(BF16)
+            along_x(lambda to: rows_of(middle, 256 + to * 16, 16), lambda i: c_x.at[b, i], 3)
+
+        def spread_parts():
+            wait_bytes(a_z.at[b], r_recv.at[b, 2])
+            mine = pl.ds(aligned(x * 256 + z * 32, 16), 32)
+            own = middle[pl.ds(aligned(z * 32, 16), 32), :]
+            summed[b, mine, :] = add(own, a_z[b]).astype(BF16)
+            along_z(lambda to: summed.at[b, mine], lambda i: summed.at[b, mine], 4)
+            wait_bytes(c_x.at[b], r_recv.at[b, 3])
+            last = pl.ds(aligned(1024 + z * 64 + x * 16, 16), 16)
+            own = middle[pl.ds(aligned(256 + x * 16, 16), 16), :]
+            summed[b, last, :] = add(own, c_x[b]).astype(BF16)
+            along_x(lambda to: summed.at[b, last], lambda i: summed.at[b, last], 5)
+
+        def collect_parts():
+            wait_bytes(summed.at[b, pl.ds(0, 32 * (NZ - 1))], r_recv.at[b, 4])
+            mine = pl.ds(aligned(x * 256, 16), 256)
+            along_x(lambda to: summed.at[b, mine], lambda i: summed.at[b, mine], 6)
+            wait_bytes(summed.at[b, pl.ds(0, 16 * (NX - 1))], r_recv.at[b, 5])
+            last = pl.ds(aligned(1024 + z * 64, 16), 64)
+            along_z(lambda to: summed.at[b, last], lambda i: summed.at[b, last], 7)
 
         def attend_rows(i, carry):
             @pl.when(i == 1)
@@ -432,9 +464,12 @@
             return carry
 
         lax.fori_loop(0, length // 1024, attend_rows, 0)
+        spread_parts()
         output_forward(b)
-
-        wait_bytes(summed.at[b, pl.ds(0, 48 * (NV - 1))], r_recv.at[b, 1])
+        collect_parts()
+
+        wait_bytes(summed.at[b, pl.ds(0, 256 * (NX - 1))], r_recv.at[b, 6])
+        wait_bytes(summed.at[b, pl.ds(0, 64 * (NZ - 1))], r_recv.at[b, 7])
 
         @pl.when(b == 0)
         def _():
@@ -525,8 +560,8 @@
                 launch_tokens(b + 1, part)
 
         wait_bytes(to_mix.at[pl.ds(0, tokens * (NH - 1))], m_send.at[b])
-        wait_bytes(to_sum.at[pl.ds(0, 48 * (NV - 1))], r_send.at[b, 0])
-        wait_bytes(summed.at[b, pl.ds(0, 48 * (NV - 1))], r_send.at[b, 1])
+        for sem, count in enumerate((768, 448, 224, 48, 224, 48, 768, 448)):
+            wait_bytes(summed.at[b, pl.ds(0, count)], r_send.at[b, sem])
         wait_bytes(gathered.at[b, pl.ds(0, tokens * 7)], g_send.at[b])
         wait_bytes(out_w.at[b, pl.ds(0, 128 * 7)], og_send.at[b])
         return carry
@@ -553,7 +588,6 @@
 def shards(features, attend_weight, output_weight, fast_init, update_mask):
     tokens, width = features.shape
     length = tokens * NH
-    pieces = jnp.transpose(fast_init, (0, 2, 4, 1, 3)).reshape(BLOCKS, 3, 16, 128)
     vmem = pl.BlockSpec(memory_space=pltpu.VMEM)
     dma = pltpu.SemaphoreType.DMA
     return pl.pallas_call(
@@ -574,7 +608,11 @@
             pltpu.VMEM((3, 1024, 128), BF16),
             pltpu.VMEM((3, 512, 128), F32),
             pltpu.VMEM((1536, 128), BF16),
-            pltpu.VMEM((BLOCKS, NV - 1, 48, 128), BF16),
+            pltpu.VMEM((BLOCKS, NX - 1, 256, 128), BF16),
+            pltpu.VMEM((BLOCKS, NZ - 1, 64, 128), BF16),
+            pltpu.VMEM((BLOCKS, NZ - 1, 32, 128), BF16),
+            pltpu.VMEM((BLOCKS, NX - 1, 16, 128), BF16),
+            pltpu.VMEM((320, 128), BF16),
             pltpu.VMEM((BLOCKS, 1536, 128), BF16),
             pltpu.VMEM((length, 128), F32),
             pltpu.VMEM((length, 128), BF16),
@@ -587,8 +625,8 @@
             dma((BLOCKS,)),
             dma((BLOCKS, 12)),
             dma((BLOCKS,)),
-            dma((BLOCKS, 2)),
-            dma((BLOCKS, 2)),
+            dma((BLOCKS, 8)),
+            dma((BLOCKS, 8)),
             dma((BLOCKS, 2)),
             dma((BLOCKS,)),
         ],
@@ -596,7 +634,7 @@
             collective_id=0, has_side_effects=True, vmem_limit_bytes=56 * 1024 * 1024
         ),
         name="lact",
-    )(features, attend_weight, pieces, output_weight, update_mask)
+    )(features, attend_weight, jnp.swapaxes(fast_init, 3, 4), output_weight, update_mask)
 
 
 def solution(mesh):

time: 146 us -> 139 us (0.952)
  Pallas kernels: 142 us -> 137 us
  local copies, waits for them, and re-layouts: 3.41 us -> 1.87 us
    pallas_call x1, Pallas kernels: 142 us -> 137 us  [shards(): pl.pallas_call(kernel, out_shape=jax.ShapeDtypeStruct((tokens, width), BF...]
where the time goes in v4:
time: 139 us
  Pallas kernels  137 us (99%)
  local copies, waits for them, and re-layouts  1.87 us (1%)
    pallas_call x1, Pallas kernels, shards(): pl.pallas_call(kernel, out_shape=jax.ShapeDtypeStruct((tokens, width), BF...  137 us

profile of v4, /device:TPU:1, one launch (start us, length us, event | category | flops | bytes accessed | tf_op | source)
XLA Modules:
  0.0 139.3 jit_solution(18266273913740873737)
XLA Ops:
  0.0 137.4 %lact.1 = bf16[256,1024]{1,0:T(8,128)(2,1)} custom-call(bf16[256,1024]{1,0:T(8,128)(2,1)} %features.1, bf16[2,3,32,128]{3,2,1,0:T(8,128)(2,1)} %attend.1, bf16[2,2,3,16,64]{4,3,2,1,0:T(8,128)(2,1)} %bitcast.1, bf16[2,32,1024]{2,1,0:T(8,128)(2,1)} %outw.1, s32[1,2048]{1,0:T(1,128)} %mask.1), custom_call_target="tpu_custom_call" | custom-call | tf_op jit(solution)/shard_map/lact/pallas_call | solution.py:593
  137.4 1.9 %copy.7 = bf16[256,1024]{1,0:T(8,128)(2,1)} copy(bf16[256,1024]{1,0:T(8,128)(2,1)} %lact.1) | data formatting | bytes 1048576

commit v5 on v4

--- a/solution.py
+++ b/solution.py
@@ -274,18 +274,13 @@
     fast_z(0)
 
     def block(b, carry):
+        def forward_opposite(part):
+            wait_bytes(tokens_of(b, opposite, part).at[:, 0:512], g_recv.at[b, 7 + part])
+            wait_bytes(tokens_of(b, opposite, part).at[:, 512:1024], g_recv.at[b, 9 + part])
+            send_tokens(b, opposite, part, 11, sib)
+
         def project(s):
-            @pl.when(s == 0)
-            def _():
-                wait_bytes(tokens_of(b, sib), g_recv.at[b, 4])
-                for part, columns in enumerate(COLUMNS):
-                    wait_bytes(qkv_w.at[b, pl.ds(0, 256 * (NX - 1)), columns], w_recv.at[b, 2 + part])
-
-                @pl.when(b == 0)
-                def _():
-                    output_fetch()
-
-            @pl.when(s == 1)
+            @pl.when(s == b)
             def _():
                 for part in range(2):
                     wait_bytes(tokens_of(b, left, part), g_recv.at[b, part])
@@ -294,6 +289,19 @@
                     send_tokens(b, right, part, 9 + part, left, slice(512, 1024))
                     send_tokens(b, right, part, 5, sib)
                     send_tokens(b, left, part, 6, sib)
+
+            @pl.when(s == 0)
+            def _():
+                wait_bytes(tokens_of(b, sib), g_recv.at[b, 4])
+                for part, columns in enumerate(COLUMNS):
+                    wait_bytes(qkv_w.at[b, pl.ds(0, 256 * (NX - 1)), columns], w_recv.at[b, 2 + part])
+
+                @pl.when(b == 0)
+                def _():
+                    output_fetch()
+
+            @pl.when(s == 1)
+            def _():
                 wait_bytes(tokens_of(b, sib), g_recv.at[b, 5])
 
             @pl.when(s == 2)
@@ -302,10 +310,7 @@
 
             @pl.when(s == 3)
             def _():
-                for part in range(2):
-                    wait_bytes(tokens_of(b, opposite, part).at[:, 0:512], g_recv.at[b, 7 + part])
-                    wait_bytes(tokens_of(b, opposite, part).at[:, 512:1024], g_recv.at[b, 9 + part])
-                    send_tokens(b, opposite, part, 11, sib)
+                forward_opposite(1)
                 wait_bytes(tokens_of(b, sib), g_recv.at[b, 11])
 
             rows = pl.ds(aligned(((y + gray(s)) % NY) * pair, pair), pair)
@@ -338,6 +343,10 @@
                     low = low_lanes(weights.shape)
                     wide[j, 0:512, :] = jnp.where(low, weights, jnp.zeros_like(weights))
                     wide[j, 512:1024, :] = jnp.where(low, jnp.zeros_like(weights), weights)
+
+            @pl.when(s == 2)
+            def _():
+                forward_opposite(0)
 
             rows = pl.ds(aligned(((y + gray(s)) % NY) * pair, pair), pair)
             k = keys[rows, :]

time: 139 us -> 139 us (level)
  no operation moved by 1% of the time
where the time goes in v5:
time: 139 us; the launch traced here: 138 us
  Pallas kernels  136 us (98%)
  local copies, waits for them, and re-layouts  1.87 us (1%)
    pallas_call x1, Pallas kernels, shards(): pl.pallas_call(kernel, out_shape=jax.ShapeDtypeStruct((tokens, width), BF...  136 us

profile of v5, /device:TPU:1, one launch (start us, length us, event | category | flops | bytes accessed | tf_op | source)
XLA Modules:
  0.0 138.4 jit_solution(18233370321863879638)
XLA Ops:
  0.0 136.5 %lact.1 = bf16[256,1024]{1,0:T(8,128)(2,1)} custom-call(bf16[256,1024]{1,0:T(8,128)(2,1)} %features.1, bf16[2,3,32,128]{3,2,1,0:T(8,128)(2,1)} %attend.1, bf16[2,2,3,16,64]{4,3,2,1,0:T(8,128)(2,1)} %bitcast.1, bf16[2,32,1024]{2,1,0:T(8,128)(2,1)} %outw.1, s32[1,2048]{1,0:T(1,128)} %mask.1), custom_call_target="tpu_custom_call" | custom-call | tf_op jit(solution)/shard_map/lact/pallas_call | solution.py:602
  136.5 1.9 %copy.7 = bf16[256,1024]{1,0:T(8,128)(2,1)} copy(bf16[256,1024]{1,0:T(8,128)(2,1)} %lact.1) | data formatting | bytes 1048576

commit v6 on v5

--- a/solution.py
+++ b/solution.py
@@ -232,8 +232,8 @@
 
     group = view // 4
 
-    def output_fetch():
-        rows = pl.ds(aligned(view * 32, 32), 32)
+    def output_fetch(b):
+        target = out_w.at[b, pl.ds(aligned(view * 32, 32), 32)]
         target_group = (group - head + NH) % NH
 
         def send(i, carry):
@@ -241,11 +241,11 @@
 
             @pl.when(to == view)
             def _():
-                pltpu.make_async_copy(outw, out_w.at[:, rows], o_recv).start()
+                pltpu.make_async_copy(outw.at[b], target, o_recv.at[b]).start()
 
             @pl.when(to != view)
             def _():
-                start_copy(outw, out_w.at[:, rows], o_send, o_recv, to, head)
+                start_copy(outw.at[b], target, o_send.at[b], o_recv.at[b], to, head)
 
             return carry
 
@@ -295,10 +295,6 @@
                 wait_bytes(tokens_of(b, sib), g_recv.at[b, 4])
                 for part, columns in enumerate(COLUMNS):
                     wait_bytes(qkv_w.at[b, pl.ds(0, 256 * (NX - 1)), columns], w_recv.at[b, 2 + part])
-
-                @pl.when(b == 0)
-                def _():
-                    output_fetch()
 
             @pl.when(s == 1)
             def _():
@@ -334,6 +330,7 @@
 
                 @pl.when(b == 0)
                 def _():
+                    output_fetch(0)
                     projections_z(1)
                     fast_x(1)
 
@@ -416,12 +413,6 @@
         along_x(lambda to: rows_of(to_sum, to * 256, 256), lambda i: a_x.at[b, i], 0)
         along_z(lambda to: rows_of(to_sum, 1024 + to * 64, 64), lambda i: c_z.at[b, i], 1)
 
-        @pl.when(b == 0)
-        def _():
-            wait_bytes(out_w.at[:, pl.ds(0, 128)], o_recv)
-
-        output_share(b)
-
         def reduce_parts():
             wait_bytes(a_x.at[b], r_recv.at[b, 0])
             own = to_sum[pl.ds(aligned(x * 256, 16), 256), :]
@@ -456,6 +447,8 @@
             @pl.when(i == 1)
             def _():
                 reduce_parts()
+                wait_bytes(out_w.at[b, pl.ds(0, 128)], o_recv.at[b])
+                output_share(b)
 
             rows = pl.ds(aligned(i * 1024, 1024), 1024)
             q = scaled[rows, :]
@@ -474,16 +467,17 @@
 
         lax.fori_loop(0, length // 1024, attend_rows, 0)
         spread_parts()
-        output_forward(b)
         collect_parts()
 
         wait_bytes(summed.at[b, pl.ds(0, 256 * (NX - 1))], r_recv.at[b, 6])
         wait_bytes(summed.at[b, pl.ds(0, 64 * (NZ - 1))], r_recv.at[b, 7])
+        output_forward(b)
 
         @pl.when(b == 0)
         def _():
             projections_x(1)
             fast_z(1)
+            output_fetch(1)
 
         row = lax.broadcasted_iota(jnp.int32, (128, 128), 0)
         col = lax.broadcasted_iota(jnp.int32, (128, 128), 1)
@@ -587,11 +581,13 @@
 
     @pl.when(head == 0)
     def _():
-        wait_bytes(out_w.at[:, pl.ds(0, 96)], o_send)
+        for b in range(BLOCKS):
+            wait_bytes(out_w.at[b, pl.ds(0, 96)], o_send.at[b])
 
     @pl.when(head != 0)
     def _():
-        wait_bytes(out_w.at[:, pl.ds(0, 128)], o_send)
+        for b in range(BLOCKS):
+            wait_bytes(out_w.at[b, pl.ds(0, 128)], o_send.at[b])
 
 
 def shards(features, attend_weight, output_weight, fast_init, update_mask):
@@ -628,8 +624,8 @@
             pltpu.VMEM((BLOCKS, tokens, width), BF16),
             dma((BLOCKS, 6)),
             dma((BLOCKS, 6)),
-            dma,
-            dma,
+            dma((BLOCKS,)),
+            dma((BLOCKS,)),
             dma((BLOCKS, 2)),
             dma((BLOCKS,)),
             dma((BLOCKS, 12)),

time: 139 us -> 138 us (level)
  no operation moved by 1% of the time
where the time goes in v6:
time: 138 us
  Pallas kernels  136 us (99%)
  local copies, waits for them, and re-layouts  1.87 us (1%)
    pallas_call x1, Pallas kernels, shards(): pl.pallas_call(kernel, out_shape=jax.ShapeDtypeStruct((tokens, width), BF...  136 us

profile of v6, /device:TPU:1, one launch (start us, length us, event | category | flops | bytes accessed | tf_op | source)
XLA Modules:
  0.0 138.0 jit_solution(776217588466355518)
XLA Ops:
  0.0 136.1 %lact.1 = bf16[256,1024]{1,0:T(8,128)(2,1)} custom-call(bf16[256,1024]{1,0:T(8,128)(2,1)} %features.1, bf16[2,3,32,128]{3,2,1,0:T(8,128)(2,1)} %attend.1, bf16[2,2,3,16,64]{4,3,2,1,0:T(8,128)(2,1)} %bitcast.1, bf16[2,32,1024]{2,1,0:T(8,128)(2,1)} %outw.1, s32[1,2048]{1,0:T(1,128)} %mask.1), custom_call_target="tpu_custom_call" | custom-call | tf_op jit(solution)/shard_map/lact/pallas_call | solution.py:598
  136.1 1.9 %copy.7 = bf16[256,1024]{1,0:T(8,128)(2,1)} copy(bf16[256,1024]{1,0:T(8,128)(2,1)} %lact.1) | data formatting | bytes 1048576

commit v7 on v6

--- a/solution.py
+++ b/solution.py
@@ -493,7 +493,7 @@
             scales.append(scale)
             grams.append(gram * (scale * scale))
         for step in range(NS_STEPS):
-            product = exact if step < 2 else triple
+            product = exact if step < 1 else triple
             polys = [
                 jnp.where(eye, NEWTON[0], 0.0)
                 + NEWTON[1] * gram

time: 138 us -> 138 us (level)
  no operation moved by 1% of the time
where the time goes in v7:
time: 138 us
  Pallas kernels  136 us (99%)
  local copies, waits for them, and re-layouts  1.87 us (1%)
    pallas_call x1, Pallas kernels, shards(): pl.pallas_call(kernel, out_shape=jax.ShapeDtypeStruct((tokens, width), BF...  136 us

profile of v7, /device:TPU:1, one launch (start us, length us, event | category | flops | bytes accessed | tf_op | source)
XLA Modules:
  0.0 137.7 jit_solution(18077965262886983254)
XLA Ops:
  0.0 135.8 %lact.1 = bf16[256,1024]{1,0:T(8,128)(2,1)} custom-call(bf16[256,1024]{1,0:T(8,128)(2,1)} %features.1, bf16[2,3,32,128]{3,2,1,0:T(8,128)(2,1)} %attend.1, bf16[2,2,3,16,64]{4,3,2,1,0:T(8,128)(2,1)} %bitcast.1, bf16[2,32,1024]{2,1,0:T(8,128)(2,1)} %outw.1, s32[1,2048]{1,0:T(1,128)} %mask.1), custom_call_target="tpu_custom_call" | custom-call | tf_op jit(solution)/shard_map/lact/pallas_call | solution.py:598
  135.8 1.9 %copy.7 = bf16[256,1024]{1,0:T(8,128)(2,1)} copy(bf16[256,1024]{1,0:T(8,128)(2,1)} %lact.1) | data formatting | bytes 1048576
